TPU v7x, 32 devices: a whole 2x2x4 slice. The times are simulated.
32 devices in a mesh: src: 8 (over y, x, core), tgt: 4 (over z).
Axes of the slice: x: 2, y: 2, z: 4, core: 2. Of those that a mesh axis runs over, the one named last changes fastest.
Arguments:
- feature_a: bfloat16 [16, 128, 1024], P('src', 'tgt'), may hold values from -6 to 6
- feature_b: bfloat16 [8, 16, 1024], P('tgt', 'src'), may hold values from -6 to 6
- conv_in: float32 [8, 81], replicated, may hold values from -0.625 to 0.625
- bias_in: float32 [8], replicated, may hold values from -4 to 4
- conv_out: float32 [8, 81], replicated, may hold values from -0.25 to 0.25
Outputs:
- consensus: float32 [8, 16, 16, 128], P('tgt', 'src')
All inputs are finite; a program needn't handle non-finite values.
Results may differ from a plain program's by a relative error of at most 0.0024.
Values may be sent and summed in bfloat16 or wider, within the bound.
A program may use at most 64 MiB of HBM per device.

v0:
```python
import jax
import jax.numpy as jnp
from jax import lax
from jax.sharding import PartitionSpec as P


def extended_2(block, sides, width):
    for axis, dim in sides:
        count = lax.axis_size(axis)
        forward = [(i, i + 1) for i in range(count - 1)]
        backward = [(target, source) for source, target in forward]
        low = lax.ppermute(
            lax.slice_in_dim(block, block.shape[dim] - width, None, axis=dim), axis, forward
        )
        high = lax.ppermute(lax.slice_in_dim(block, 0, width, axis=dim), axis, backward)
        block = jnp.concatenate([low, block, high], axis=dim)
    return block


def filter_taps(source, weights, extent):
    summed_total = jnp.zeros(extent, jnp.float32)
    for first in range(3):
        for second in range(3):
            for third in range(3):
                for fourth in range(3):
                    weight = weights[first * 27 + second * 9 + third * 3 + fourth]
                    summed_total = (
                        summed_total
                        + weight
                        * source[
                            first : first + extent[0],
                            second : second + extent[1],
                            third : third + extent[2],
                            fourth : fourth + extent[3],
                        ]
                    )
    return summed_total


def per_device(feature_a, feature_b, conv_in, bias_in, conv_out):
    rows_b = feature_b.shape[0]
    cols_b = feature_b.shape[1]
    channels = feature_b.shape[2]
    feature_b = extended_2(feature_b, (("src", 1), ("tgt", 0)), 2)
    ext_r = feature_b.shape[0]
    ext_c = feature_b.shape[1]
    flat_b = feature_b.reshape(ext_r * ext_c, channels)
    wide = lax.all_gather(feature_a, "tgt", axis=1, tiled=True)
    piece = lax.all_gather(wide, "src", axis=0, tiled=True)
    count_r = piece.shape[0]
    count_c = piece.shape[1]
    scores = jnp.einsum(
        "qc,pc->qp",
        flat_b,
        piece.reshape(count_r * count_c, channels),
        preferred_element_type=jnp.float32,
    )
    scores = (scores * channels ** (-0.5)).astype(jnp.bfloat16)
    volume = scores.reshape(ext_r, ext_c, count_r, count_c)
    source_rows = volume.shape[2]
    source_cols = volume.shape[3]
    border_padding = ((0, 0), (0, 0), (1, 1), (1, 1))
    field = jnp.pad(volume.astype(jnp.float32), border_padding)
    total_r = rows_b * lax.axis_size("tgt")
    total_c = cols_b * lax.axis_size("src")
    index_r = lax.axis_index("tgt") * rows_b - 1 + jnp.arange(rows_b + 2, dtype=jnp.int32)
    index_c = lax.axis_index("src") * cols_b - 1 + jnp.arange(cols_b + 2, dtype=jnp.int32)
    inside_r = ((index_r >= 0) & (index_r < total_r)).astype(jnp.float32)
    inside_c = ((index_c >= 0) & (index_c < total_c)).astype(jnp.float32)
    inside = inside_r[:, None, None, None] * inside_c[None, :, None, None]
    hidden_count = conv_in.shape[0]
    mirror_in = (
        conv_in.reshape(hidden_count, 3, 3, 3, 3).transpose(0, 3, 4, 1, 2).reshape(hidden_count, 81)
    )
    reflected_output = (
        conv_out.reshape(hidden_count, 3, 3, 3, 3)
        .transpose(0, 3, 4, 1, 2)
        .reshape(hidden_count, 81)
    )
    extended = (rows_b + 2, cols_b + 2, source_rows, source_cols)
    local_entries = (rows_b, cols_b, source_rows, source_cols)

    def channel_step(channel_slot, summed_total):
        hidden_fwd = (
            jax.nn.relu(filter_taps(field, conv_in[channel_slot], extended) + bias_in[channel_slot])
            * inside
        )
        hidden_reflected = (
            jax.nn.relu(
                filter_taps(field, mirror_in[channel_slot], extended) + bias_in[channel_slot]
            )
            * inside
        )
        summed_total = summed_total + filter_taps(
            jnp.pad(hidden_fwd, border_padding), conv_out[channel_slot], local_entries
        )
        return summed_total + filter_taps(
            jnp.pad(hidden_reflected, border_padding), reflected_output[channel_slot], local_entries
        )

    return lax.fori_loop(0, hidden_count, channel_step, jnp.zeros(local_entries, jnp.float32))


def solution(mesh):
    in_specs = (P("src", "tgt", None), P("tgt", "src", None), P(), P(), P())
    out_specs = P("tgt", "src", None, None)
    return jax.shard_map(
        per_device, mesh=mesh, in_specs=in_specs, out_specs=out_specs, check_vma=False
    )
```

profile of v0, /device:TPU:1, one launch (start us, length us, event | category | flops | bytes accessed | tf_op | source)
XLA Modules:
  0.0 1864.2 jit_solution(1072556854888386898)
XLA Ops:
  6.5 16.5 all_gather.6
  23.1 6.0 collective-permute-start
  29.1 1.9 collective-permute-start.1
  31.1 3.2 collective-permute-done.1
  35.0 1.7 collective-permute-start.2
  36.8 1.3 collective-permute-start.3
  38.1 0.8 copy.14
  39.0 0.8 copy.16
  40.0 1.9 collective-permute-done.3
  41.8 0.7 pad_maximum_fusion
  42.6 19.8 %all-gather.2.cloned.1.call-done = bf16[16,128,1024]{2,1,0:T(8,128)(2,1)} async-done(((bf16[2,128,1024]{2,1,0:T(8,128)(2,1)}), bf16[16,128,1024]{2,1,0:T(8,128)(2,1)}) %all-gather.2.cloned.1.call-update) | async-done | bytes 4194320 | tf_op jit(solution)/shard_map/all_gather | solution.py:49
  62.4 3.5 fusion.308
  66.3 1790.4 %while.16 = (s32[]{:T(128)}, f32[2,2,16,128]{3,2,1,0:T(8,128)S(1)}, f32[8,81]{1,0:T(8,128)}, f32[8,81]{1,0:T(8,128)}, f32[6,6,18,130]{3,2,1,0:T(8,128)S(1)}, /*i...) while((s32[]{:T(128)}, f32[2,2,16,128]{3,2,1,0:T(8,128)S(1)}, ...), condition=%wide.region_1.2_spmd.clone, body=%wide.region_0.1_spmd.clone.sunk | while | flops 13410323 | bytes 22420168 | solution.py:101
  68.5 0.7 fusion.360
  70.6 53.0 %maximum_multiply_fusion.5 = f32[4,4,16,128]{3,2,1,0:T(8,128)S(1)} fusion(f32[6,6,18,130]{3,2,1,0:T(8,128)S(1)} %get-tuple-element.1378, f32[]{:T(128)} %bitcast.753, f32[]{:T(128)} %bitcast.754, f32[]{:T(128)} %bitcast.755, f32[]{:T(128)} %bitcast.756, f32[]{:T(128)} %bitcast.757, f32[]{:T(128)} %bitcast.758, f32[]{:T(128)} %bitcast.759, ...), kind=kLoop, calls=%fused_computation.145.clone.1 | loop fusion | flops 5373952 | bytes 10748296 | tf_op jit(solution)/shard_map/while/body/eval_jaxpr/mul | solution.py:89
  126.5 0.7 fusion.355
  127.9 53.0 %maximum_multiply_fusion.4 = f32[4,4,16,128]{3,2,1,0:T(8,128)S(1)} fusion(f32[6,6,18,130]{3,2,1,0:T(8,128)S(1)} %get-tuple-element.1378, f32[4,4]{1,0:T(4,128)S(1)} %multiply_bitcast_fusion.2, f32[]{:T(128)} %bitcast.671, f32[]{:T(128)} %bitcast.672, f32[]{:T(128)} %bitcast.673, f32[]{:T(128)} %bitcast.674, f32[]{:T(128)} %bitcast.675, ...), kind=kLoop, calls=%fused_computation.146.clone.1 | loop fusion | flops 5373952 | bytes 10748296 | tf_op jit(solution)/shard_map/while/body/eval_jaxpr/mul | solution.py:85
  185.3 0.7 fusion.369
  186.0 0.7 fusion.370
  188.1 102.0 %fusion.372 = f32[2,2,16,128]{3,2,1,0:T(8,128)S(1)} fusion(f32[4,4,16,128]{3,2,1,0:T(8,128)S(1)} %maximum_multiply_fusion.4, f32[4,4,16,128]{3,2,1,0:T(8,128)S(1)} %maximum_multiply_fusion.5, f32[2,2,16,128]{3,2,1,0:T(8,128)S(1)} %get-tuple-element.1363, f32[]{:T(128)} %bitcast.834, f32[]{:T(128)} %bitcast.835, f32[]{:T(128)} %bitcast.836, ...), kind=kLoop, calls=%fused_computation.294.clone.1 | loop fusion | flops 2662400 | bytes 918153 | tf_op jit(solution)/shard_map/while/body/eval_jaxpr/add | solution.py:97
  292.3 0.7 fusion.360
  294.4 53.0 %maximum_multiply_fusion.5 = f32[4,4,16,128]{3,2,1,0:T(8,128)S(1)} fusion(f32[6,6,18,130]{3,2,1,0:T(8,128)S(1)} %get-tuple-element.1378, f32[]{:T(128)} %bitcast.753, f32[]{:T(128)} %bitcast.754, f32[]{:T(128)} %bitcast.755, f32[]{:T(128)} %bitcast.756, f32[]{:T(128)} %bitcast.757, f32[]{:T(128)} %bitcast.758, f32[]{:T(128)} %bitcast.759, ...), kind=kLoop, calls=%fused_computation.145.clone.1 | loop fusion | flops 5373952 | bytes 10748296 | tf_op jit(solution)/shard_map/while/body/eval_jaxpr/mul | solution.py:89
  351.7 53.0 %maximum_multiply_fusion.4 = f32[4,4,16,128]{3,2,1,0:T(8,128)S(1)} fusion(f32[6,6,18,130]{3,2,1,0:T(8,128)S(1)} %get-tuple-element.1378, f32[4,4]{1,0:T(4,128)S(1)} %multiply_bitcast_fusion.2, f32[]{:T(128)} %bitcast.671, f32[]{:T(128)} %bitcast.672, f32[]{:T(128)} %bitcast.673, f32[]{:T(128)} %bitcast.674, f32[]{:T(128)} %bitcast.675, ...), kind=kLoop, calls=%fused_computation.146.clone.1 | loop fusion | flops 5373952 | bytes 10748296 | tf_op jit(solution)/shard_map/while/body/eval_jaxpr/mul | solution.py:85
  409.1 0.7 fusion.369
  409.8 0.7 fusion.370
  411.9 102.0 %fusion.372 = f32[2,2,16,128]{3,2,1,0:T(8,128)S(1)} fusion(f32[4,4,16,128]{3,2,1,0:T(8,128)S(1)} %maximum_multiply_fusion.4, f32[4,4,16,128]{3,2,1,0:T(8,128)S(1)} %maximum_multiply_fusion.5, f32[2,2,16,128]{3,2,1,0:T(8,128)S(1)} %get-tuple-element.1363, f32[]{:T(128)} %bitcast.834, f32[]{:T(128)} %bitcast.835, f32[]{:T(128)} %bitcast.836, ...), kind=kLoop, calls=%fused_computation.294.clone.1 | loop fusion | flops 2662400 | bytes 918153 | tf_op jit(solution)/shard_map/while/body/eval_jaxpr/add | solution.py:97
  518.2 53.0 %maximum_multiply_fusion.5 = f32[4,4,16,128]{3,2,1,0:T(8,128)S(1)} fusion(f32[6,6,18,130]{3,2,1,0:T(8,128)S(1)} %get-tuple-element.1378, f32[]{:T(128)} %bitcast.753, f32[]{:T(128)} %bitcast.754, f32[]{:T(128)} %bitcast.755, f32[]{:T(128)} %bitcast.756, f32[]{:T(128)} %bitcast.757, f32[]{:T(128)} %bitcast.758, f32[]{:T(128)} %bitcast.759, ...), kind=kLoop, calls=%fused_computation.145.clone.1 | loop fusion | flops 5373952 | bytes 10748296 | tf_op jit(solution)/shard_map/while/body/eval_jaxpr/mul | solution.py:89
  574.1 0.7 fusion.355
  575.5 53.0 %maximum_multiply_fusion.4 = f32[4,4,16,128]{3,2,1,0:T(8,128)S(1)} fusion(f32[6,6,18,130]{3,2,1,0:T(8,128)S(1)} %get-tuple-element.1378, f32[4,4]{1,0:T(4,128)S(1)} %multiply_bitcast_fusion.2, f32[]{:T(128)} %bitcast.671, f32[]{:T(128)} %bitcast.672, f32[]{:T(128)} %bitcast.673, f32[]{:T(128)} %bitcast.674, f32[]{:T(128)} %bitcast.675, ...), kind=kLoop, calls=%fused_computation.146.clone.1 | loop fusion | flops 5373952 | bytes 10748296 | tf_op jit(solution)/shard_map/while/body/eval_jaxpr/mul | solution.py:85
  632.9 0.7 fusion.369
  633.6 0.7 fusion.370
  635.7 102.0 %fusion.372 = f32[2,2,16,128]{3,2,1,0:T(8,128)S(1)} fusion(f32[4,4,16,128]{3,2,1,0:T(8,128)S(1)} %maximum_multiply_fusion.4, f32[4,4,16,128]{3,2,1,0:T(8,128)S(1)} %maximum_multiply_fusion.5, f32[2,2,16,128]{3,2,1,0:T(8,128)S(1)} %get-tuple-element.1363, f32[]{:T(128)} %bitcast.834, f32[]{:T(128)} %bitcast.835, f32[]{:T(128)} %bitcast.836, ...), kind=kLoop, calls=%fused_computation.294.clone.1 | loop fusion | flops 2662400 | bytes 918153 | tf_op jit(solution)/shard_map/while/body/eval_jaxpr/add | solution.py:97
  739.9 0.7 fusion.360
  742.0 53.0 %maximum_multiply_fusion.5 = f32[4,4,16,128]{3,2,1,0:T(8,128)S(1)} fusion(f32[6,6,18,130]{3,2,1,0:T(8,128)S(1)} %get-tuple-element.1378, f32[]{:T(128)} %bitcast.753, f32[]{:T(128)} %bitcast.754, f32[]{:T(128)} %bitcast.755, f32[]{:T(128)} %bitcast.756, f32[]{:T(128)} %bitcast.757, f32[]{:T(128)} %bitcast.758, f32[]{:T(128)} %bitcast.759, ...), kind=kLoop, calls=%fused_computation.145.clone.1 | loop fusion | flops 5373952 | bytes 10748296 | tf_op jit(solution)/shard_map/while/body/eval_jaxpr/mul | solution.py:89
  797.9 0.7 fusion.355
  799.3 53.0 %maximum_multiply_fusion.4 = f32[4,4,16,128]{3,2,1,0:T(8,128)S(1)} fusion(f32[6,6,18,130]{3,2,1,0:T(8,128)S(1)} %get-tuple-element.1378, f32[4,4]{1,0:T(4,128)S(1)} %multiply_bitcast_fusion.2, f32[]{:T(128)} %bitcast.671, f32[]{:T(128)} %bitcast.672, f32[]{:T(128)} %bitcast.673, f32[]{:T(128)} %bitcast.674, f32[]{:T(128)} %bitcast.675, ...), kind=kLoop, calls=%fused_computation.146.clone.1 | loop fusion | flops 5373952 | bytes 10748296 | tf_op jit(solution)/shard_map/while/body/eval_jaxpr/mul | solution.py:85
  856.7 0.7 fusion.369
  857.4 0.7 fusion.370
  859.5 102.0 %fusion.372 = f32[2,2,16,128]{3,2,1,0:T(8,128)S(1)} fusion(f32[4,4,16,128]{3,2,1,0:T(8,128)S(1)} %maximum_multiply_fusion.4, f32[4,4,16,128]{3,2,1,0:T(8,128)S(1)} %maximum_multiply_fusion.5, f32[2,2,16,128]{3,2,1,0:T(8,128)S(1)} %get-tuple-element.1363, f32[]{:T(128)} %bitcast.834, f32[]{:T(128)} %bitcast.835, f32[]{:T(128)} %bitcast.836, ...), kind=kLoop, calls=%fused_computation.294.clone.1 | loop fusion | flops 2662400 | bytes 918153 | tf_op jit(solution)/shard_map/while/body/eval_jaxpr/add | solution.py:97
  963.7 0.7 fusion.360
  965.8 53.0 %maximum_multiply_fusion.5 = f32[4,4,16,128]{3,2,1,0:T(8,128)S(1)} fusion(f32[6,6,18,130]{3,2,1,0:T(8,128)S(1)} %get-tuple-element.1378, f32[]{:T(128)} %bitcast.753, f32[]{:T(128)} %bitcast.754, f32[]{:T(128)} %bitcast.755, f32[]{:T(128)} %bitcast.756, f32[]{:T(128)} %bitcast.757, f32[]{:T(128)} %bitcast.758, f32[]{:T(128)} %bitcast.759, ...), kind=kLoop, calls=%fused_computation.145.clone.1 | loop fusion | flops 5373952 | bytes 10748296 | tf_op jit(solution)/shard_map/while/body/eval_jaxpr/mul | solution.py:89
  1021.7 0.7 fusion.355
  1023.1 53.0 %maximum_multiply_fusion.4 = f32[4,4,16,128]{3,2,1,0:T(8,128)S(1)} fusion(f32[6,6,18,130]{3,2,1,0:T(8,128)S(1)} %get-tuple-element.1378, f32[4,4]{1,0:T(4,128)S(1)} %multiply_bitcast_fusion.2, f32[]{:T(128)} %bitcast.671, f32[]{:T(128)} %bitcast.672, f32[]{:T(128)} %bitcast.673, f32[]{:T(128)} %bitcast.674, f32[]{:T(128)} %bitcast.675, ...), kind=kLoop, calls=%fused_computation.146.clone.1 | loop fusion | flops 5373952 | bytes 10748296 | tf_op jit(solution)/shard_map/while/body/eval_jaxpr/mul | solution.py:85
  1080.5 0.7 fusion.369
  1081.2 0.7 fusion.370
  1083.3 102.0 %fusion.372 = f32[2,2,16,128]{3,2,1,0:T(8,128)S(1)} fusion(f32[4,4,16,128]{3,2,1,0:T(8,128)S(1)} %maximum_multiply_fusion.4, f32[4,4,16,128]{3,2,1,0:T(8,128)S(1)} %maximum_multiply_fusion.5, f32[2,2,16,128]{3,2,1,0:T(8,128)S(1)} %get-tuple-element.1363, f32[]{:T(128)} %bitcast.834, f32[]{:T(128)} %bitcast.835, f32[]{:T(128)} %bitcast.836, ...), kind=kLoop, calls=%fused_computation.294.clone.1 | loop fusion | flops 2662400 | bytes 918153 | tf_op jit(solution)/shard_map/while/body/eval_jaxpr/add | solution.py:97
  1189.6 53.0 %maximum_multiply_fusion.5 = f32[4,4,16,128]{3,2,1,0:T(8,128)S(1)} fusion(f32[6,6,18,130]{3,2,1,0:T(8,128)S(1)} %get-tuple-element.1378, f32[]{:T(128)} %bitcast.753, f32[]{:T(128)} %bitcast.754, f32[]{:T(128)} %bitcast.755, f32[]{:T(128)} %bitcast.756, f32[]{:T(128)} %bitcast.757, f32[]{:T(128)} %bitcast.758, f32[]{:T(128)} %bitcast.759, ...), kind=kLoop, calls=%fused_computation.145.clone.1 | loop fusion | flops 5373952 | bytes 10748296 | tf_op jit(solution)/shard_map/while/body/eval_jaxpr/mul | solution.py:89
  1245.5 0.7 fusion.355
  1246.9 53.0 %maximum_multiply_fusion.4 = f32[4,4,16,128]{3,2,1,0:T(8,128)S(1)} fusion(f32[6,6,18,130]{3,2,1,0:T(8,128)S(1)} %get-tuple-element.1378, f32[4,4]{1,0:T(4,128)S(1)} %multiply_bitcast_fusion.2, f32[]{:T(128)} %bitcast.671, f32[]{:T(128)} %bitcast.672, f32[]{:T(128)} %bitcast.673, f32[]{:T(128)} %bitcast.674, f32[]{:T(128)} %bitcast.675, ...), kind=kLoop, calls=%fused_computation.146.clone.1 | loop fusion | flops 5373952 | bytes 10748296 | tf_op jit(solution)/shard_map/while/body/eval_jaxpr/mul | solution.py:85
  1304.3 0.7 fusion.369
  1305.0 0.7 fusion.370
  1307.1 102.0 %fusion.372 = f32[2,2,16,128]{3,2,1,0:T(8,128)S(1)} fusion(f32[4,4,16,128]{3,2,1,0:T(8,128)S(1)} %maximum_multiply_fusion.4, f32[4,4,16,128]{3,2,1,0:T(8,128)S(1)} %maximum_multiply_fusion.5, f32[2,2,16,128]{3,2,1,0:T(8,128)S(1)} %get-tuple-element.1363, f32[]{:T(128)} %bitcast.834, f32[]{:T(128)} %bitcast.835, f32[]{:T(128)} %bitcast.836, ...), kind=kLoop, calls=%fused_computation.294.clone.1 | loop fusion | flops 2662400 | bytes 918153 | tf_op jit(solution)/shard_map/while/body/eval_jaxpr/add | solution.py:97
  1411.3 0.7 fusion.360
  1413.4 53.0 %maximum_multiply_fusion.5 = f32[4,4,16,128]{3,2,1,0:T(8,128)S(1)} fusion(f32[6,6,18,130]{3,2,1,0:T(8,128)S(1)} %get-tuple-element.1378, f32[]{:T(128)} %bitcast.753, f32[]{:T(128)} %bitcast.754, f32[]{:T(128)} %bitcast.755, f32[]{:T(128)} %bitcast.756, f32[]{:T(128)} %bitcast.757, f32[]{:T(128)} %bitcast.758, f32[]{:T(128)} %bitcast.759, ...), kind=kLoop, calls=%fused_computation.145.clone.1 | loop fusion | flops 5373952 | bytes 10748296 | tf_op jit(solution)/shard_map/while/body/eval_jaxpr/mul | solution.py:89
  1469.3 0.7 fusion.355
  1470.7 53.0 %maximum_multiply_fusion.4 = f32[4,4,16,128]{3,2,1,0:T(8,128)S(1)} fusion(f32[6,6,18,130]{3,2,1,0:T(8,128)S(1)} %get-tuple-element.1378, f32[4,4]{1,0:T(4,128)S(1)} %multiply_bitcast_fusion.2, f32[]{:T(128)} %bitcast.671, f32[]{:T(128)} %bitcast.672, f32[]{:T(128)} %bitcast.673, f32[]{:T(128)} %bitcast.674, f32[]{:T(128)} %bitcast.675, ...), kind=kLoop, calls=%fused_computation.146.clone.1 | loop fusion | flops 5373952 | bytes 10748296 | tf_op jit(solution)/shard_map/while/body/eval_jaxpr/mul | solution.py:85
  1528.1 0.7 fusion.369
  1528.8 0.7 fusion.370
  1530.9 102.0 %fusion.372 = f32[2,2,16,128]{3,2,1,0:T(8,128)S(1)} fusion(f32[4,4,16,128]{3,2,1,0:T(8,128)S(1)} %maximum_multiply_fusion.4, f32[4,4,16,128]{3,2,1,0:T(8,128)S(1)} %maximum_multiply_fusion.5, f32[2,2,16,128]{3,2,1,0:T(8,128)S(1)} %get-tuple-element.1363, f32[]{:T(128)} %bitcast.834, f32[]{:T(128)} %bitcast.835, f32[]{:T(128)} %bitcast.836, ...), kind=kLoop, calls=%fused_computation.294.clone.1 | loop fusion | flops 2662400 | bytes 918153 | tf_op jit(solution)/shard_map/while/body/eval_jaxpr/add | solution.py:97
  1635.1 0.7 fusion.360
  1637.2 53.0 %maximum_multiply_fusion.5 = f32[4,4,16,128]{3,2,1,0:T(8,128)S(1)} fusion(f32[6,6,18,130]{3,2,1,0:T(8,128)S(1)} %get-tuple-element.1378, f32[]{:T(128)} %bitcast.753, f32[]{:T(128)} %bitcast.754, f32[]{:T(128)} %bitcast.755, f32[]{:T(128)} %bitcast.756, f32[]{:T(128)} %bitcast.757, f32[]{:T(128)} %bitcast.758, f32[]{:T(128)} %bitcast.759, ...), kind=kLoop, calls=%fused_computation.145.clone.1 | loop fusion | flops 5373952 | bytes 10748296 | tf_op jit(solution)/shard_map/while/body/eval_jaxpr/mul | solution.py:89
  1694.5 53.0 %maximum_multiply_fusion.4 = f32[4,4,16,128]{3,2,1,0:T(8,128)S(1)} fusion(f32[6,6,18,130]{3,2,1,0:T(8,128)S(1)} %get-tuple-element.1378, f32[4,4]{1,0:T(4,128)S(1)} %multiply_bitcast_fusion.2, f32[]{:T(128)} %bitcast.671, f32[]{:T(128)} %bitcast.672, f32[]{:T(128)} %bitcast.673, f32[]{:T(128)} %bitcast.674, f32[]{:T(128)} %bitcast.675, ...), kind=kLoop, calls=%fused_computation.146.clone.1 | loop fusion | flops 5373952 | bytes 10748296 | tf_op jit(solution)/shard_map/while/body/eval_jaxpr/mul | solution.py:85
  1751.9 0.7 fusion.369
  1754.7 102.0 %fusion.372 = f32[2,2,16,128]{3,2,1,0:T(8,128)S(1)} fusion(f32[4,4,16,128]{3,2,1,0:T(8,128)S(1)} %maximum_multiply_fusion.4, f32[4,4,16,128]{3,2,1,0:T(8,128)S(1)} %maximum_multiply_fusion.5, f32[2,2,16,128]{3,2,1,0:T(8,128)S(1)} %get-tuple-element.1363, f32[]{:T(128)} %bitcast.834, f32[]{:T(128)} %bitcast.835, f32[]{:T(128)} %bitcast.836, ...), kind=kLoop, calls=%fused_computation.294.clone.1 | loop fusion | flops 2662400 | bytes 918153 | tf_op jit(solution)/shard_map/while/body/eval_jaxpr/add | solution.py:97
  (188 shorter events, 107.2 us)
Async XLA Ops:
  6.5 59.8 %copy-start.1 = (f32[8]{0:T(128)S(1)}, f32[8]{0:T(128)}, u32[]{:S(2)}) copy-start(f32[8]{0:T(128)} %param.10) | copy-start | bytes 100
  6.5 55.9 %all-gather.2.cloned.1.call-start = ((), (), s32[]{:S(2)}) async-start(), calls=%async_computation | async-start | bytes 4718592 | tf_op jit(solution)/shard_map/all_gather | solution.py:49
  23.1 8.0 collective-permute-start
  29.1 5.2 collective-permute-start.1
  35.0 4.9 collective-permute-start.2
  36.8 5.1 collective-permute-start.3
  1856.7 0.6 copy-start
Sparse Core Ops, SparseCore 0:
  23.2 39.2 all-gather.1
where the time goes:
time: 1890 us; the launch traced here: 1860 us
  other arithmetic  1670 us (88%)
  local copies, waits for them, and re-layouts  127 us (7%)
  waiting for transfers between devices  25 us (1%)
    add x8, other arithmetic, channel_step(): summed_total + filter_taps(jnp.pad(hidden_reflected, border_padding), ref...  816 us
    mul x16, other arithmetic, channel_step(): jax.nn.relu(filter_taps(field, conv_in[channel_slot], extended) + bias_in...  425 us
    mul x8, other arithmetic, channel_step(): jax.nn.relu(filter_taps(field, mirror_in[channel_slot], extended) + bias_...  424 us
    slice x160, local copies, waits for them, and re-layouts, filter_taps(): weight = weights[first * 27 + second * 9 + third * 3 + fourth]  114 us
  transfers between devices with their start and end apart: 5, of which 3 were waited for; matrix products, arithmetic and copies ran while one was open for 0% of the time, Pallas kernels for 0%

commit v1 on v0

v1 whole, which is shorter than its diff:
```python
import functools

import jax
import jax.numpy as jnp
import numpy as np
from jax import lax
from jax.experimental import pallas as pl
from jax.experimental.pallas import tpu as pltpu
from jax.sharding import PartitionSpec as P

LANES = 128
F32 = jnp.float32
BF16 = jnp.bfloat16


def round_up(value, unit):
    return -(-value // unit) * unit


class Plan:
    def __init__(self, count_s, count_t, a_shape, b_shape, hidden):
        self.S, self.T = count_s, count_t
        self.rows_i, self.cols_j, self.C = a_shape
        self.kb, self.lb = b_shape[0], b_shape[1]
        self.hidden = hidden
        self.ij = self.rows_i * self.cols_j
        self.HA = self.rows_i * count_s
        self.WA = self.cols_j * count_t
        assert self.WA == LANES and LANES % self.ij == 0 and LANES // self.ij >= self.kb
        self.nk, self.nl = -(-2 // self.kb), -(-2 // self.lb)
        self.bk, self.bl = 2 * self.nk + 1, 2 * self.nl + 1
        self.L = self.bl * self.lb
        self.half = round_up(self.bk * self.L + 1, 8)
        self.KX = round_up(self.kb * self.half, 16)
        self.KP = 9 * self.KX
        self.KW = round_up(self.KP, LANES)
        self.hk, self.hl = self.kb + 2, self.lb + 2
        self.M = self.hk * self.hl * 2 * hidden
        self.unit = round_up(self.kb * self.lb, 8)
        self.Y = round_up(9 * self.unit, 16)
        assert self.Y <= LANES

    def tap(self, net, p, q, r, s):
        p, q, r, s = (p, q, r, s) if net == 0 else (r, s, p, q)
        return 27 * p + 9 * q + 3 * r + s

    def select_in(self):
        out = np.zeros((LANES, self.kb, 2, self.KW), np.float32)
        for par in range(self.kb):
            for net in range(2):
                for p, q, r, s in np.ndindex(3, 3, 3, 3):
                    ek = par + p - 2 + self.nk * self.kb
                    el = q - 2 + self.nl * self.lb
                    col = (r * 3 + s) * self.KX + (ek % self.kb) * self.half
                    col += (ek // self.kb) * self.L + el
                    out[self.tap(net, p, q, r, s), par, net, col] = 1
        return out.reshape(LANES, -1)

    def select_out(self):
        out = np.zeros((LANES, self.hk, self.hl, 2, LANES), np.float32)
        for k, l, net in np.ndindex(self.hk, self.hl, 2):
            for ok, ol, r, s in np.ndindex(self.kb, self.lb, 3, 3):
                p, q = k - ok, l - ol
                if 0 <= p < 3 and 0 <= q < 3:
                    col = (r * 3 + s) * self.unit + ok * self.lb + ol
                    out[self.tap(net, p, q, r, s), k, l, net, col] = 1
        return out.reshape(LANES, -1)


def split(x):
    high = x.astype(BF16)
    return high, (x - high.astype(F32)).astype(BF16)


def dot(x, y):
    return jnp.dot(x, y, preferred_element_type=F32)


def iota(shape, dim):
    return lax.broadcasted_iota(jnp.int32, shape, dim)


def kernel(
    g, a_hbm, b_ref, cin_ref, bias_ref, cout_ref, s1_hbm, s2_hbm, out_ref,
    a_vm, s1_vm, s2_vm, load_sem, bb, bf, vs, vp, rb, u, pat, w1h, w1l, w2h, w2l, y, cpad,
    s_a1, s_a2, r_a, s_b, r_b,
):
    S, T = g.S, g.T
    N = S * T
    s = lax.axis_index("src")
    t = lax.axis_index("tgt")
    me = s * T + t

    loads = [
        pltpu.make_async_copy(a_hbm, a_vm, load_sem.at[0]),
        pltpu.make_async_copy(s1_hbm, s1_vm, load_sem.at[1]),
        pltpu.make_async_copy(s2_hbm, s2_vm, load_sem.at[2]),
    ]
    for load in loads:
        load.start()

    barrier = pltpu.get_barrier_semaphore()

    @pl.loop(1, N)
    def _(n):
        other = lax.rem(me + n, N)
        pl.semaphore_signal(
            barrier, inc=1, device_id={"src": other // T, "tgt": lax.rem(other, T)},
            device_id_type=pl.DeviceIdType.MESH,
        )

    bb[s, t] = b_ref[...]
    vp[...] = jnp.zeros(vp.shape, BF16)
    pl.semaphore_wait(barrier, N - 1)

    def piece(ps, pt, send, ds, dt):
        return pltpu.make_async_remote_copy(
            src_ref=bb.at[ps, pt], dst_ref=bb.at[ps, pt], send_sem=send,
            recv_sem=r_a.at[ps, pt], device_id={"src": ds, "tgt": dt},
            device_id_type=pl.DeviceIdType.MESH,
        )

    def to_row(m, n):
        return piece(s, lax.rem(t + m, T), s_a2.at[m, n], lax.rem(s + n, S), t)

    def to_column(m):
        return piece(s, t, s_a1.at[m], s, lax.rem(t + m, T))

    @pl.loop(1, T)
    def _(m):
        to_column(m).start()

    @pl.loop(1, S)
    def _(n):
        to_row(0, n).start()

    @pl.loop(1, T)
    def _(m):
        piece(s, lax.rem(t + m, T), s_a1.at[m], s, lax.rem(t + m, T)).wait_recv()

        @pl.loop(1, S)
        def _(n):
            to_row(m, n).start()

    loads[1].wait()
    cpad[...] = jnp.zeros(cpad.shape, F32)
    cpad[:, : cin_ref.shape[1]] = cin_ref[...]
    taps_h, taps_l = split(cpad[...])
    both = jnp.concatenate([taps_h.astype(F32), taps_l.astype(F32)], axis=0).astype(BF16)
    base = dot(both, s1_vm[...])
    H = g.hidden
    row = iota((H, LANES), 0)
    bias = jnp.zeros((H, LANES), F32)
    for h in range(H):
        bias = jnp.where(row == h, bias_ref[h], bias)
    bias_h, bias_l = (part.astype(F32) for part in split(bias))
    bias = jnp.concatenate([bias_h, bias_h, bias_l, bias_l], axis=0)
    bias = jnp.concatenate([bias] * (g.KW // LANES), axis=1)
    bias = jnp.where(iota(bias.shape, 1) == 4 * g.KX + g.half - 1, bias, 0.0)
    for k in range(g.hk):
        at_k = t * g.kb + (k - 1)
        for l in range(g.hl):
            at_l = s * g.lb + (l - 1)
            parts = []
            for first in (0, H):
                for net in range(2):
                    at = ((k % g.kb) * 2 + net) * g.KW
                    parts.append(base[first : first + H, at : at + g.KW])
            block = jnp.concatenate(parts, axis=0)
            shift = (k // g.kb) * g.L + l
            if shift:
                block = pltpu.roll(block, shift, 1)
            inside = (at_k >= 0) & (at_k < T * g.kb) & (at_l >= 0) & (at_l < S * g.lb)
            block = (block + bias) * jnp.where(inside, 1.0, 0.0).astype(F32)
            at = (k * g.hl + l) * 2 * H
            w1h[at : at + 2 * H, :] = block[: 2 * H, : g.KP].astype(BF16)
            w1l[at : at + 2 * H, :] = block[2 * H :, : g.KP].astype(BF16)

    loads[2].wait()
    cpad[:, : cout_ref.shape[1]] = cout_ref[...]
    taps_h, taps_l = split(cpad[...])
    both = jnp.concatenate([taps_h.astype(F32), taps_l.astype(F32)], axis=0).astype(BF16)
    base = dot(both, s2_vm[...])
    blocks = g.hk * g.hl * 2
    for first, ref in ((0, w2h), (H, w2l)):
        tall = jnp.concatenate(
            [base[first : first + H, n * LANES : (n + 1) * LANES] for n in range(blocks)], axis=0
        )
        ref[...] = tall.T[: g.Y].astype(BF16)

    tail = g.half - g.bk * g.L
    u[:, g.bk * g.L :, :] = jnp.where(
        iota((T, tail, LANES), 1) == tail - 1, jnp.ones((T, tail, LANES), F32), 0.0
    )
    pat[: 3 * g.KX, LANES : 2 * LANES] = jnp.zeros((3 * g.KX, LANES), BF16)
    pat[6 * g.KX :, g.HA * LANES : (g.HA + 1) * LANES] = jnp.zeros((3 * g.KX, LANES), BF16)
    y[:, :LANES] = jnp.zeros((g.Y, LANES), F32)
    y[:, (g.HA + 1) * LANES :] = jnp.zeros((g.Y, LANES), F32)

    loads[0].wait()
    a = a_vm[...].astype(F32).reshape(g.ij, g.C)
    a = jnp.concatenate([a] * (LANES // g.ij), axis=0).astype(BF16)

    def take(ps):
        for tt in range(T):
            for kk in range(g.kb):
                bf[kk, ps, tt * g.lb : (tt + 1) * g.lb, :] = bb[ps, tt, kk].astype(F32)

    take(s)

    @pl.loop(1, S)
    def _(n):
        ps = lax.rem(s + n, S)

        @pl.loop(0, T)
        def _(m):
            pt = lax.rem(t + m, T)
            piece(ps, pt, s_a2.at[m, n], ps, t).wait_recv()

        take(ps)

    total = S * T * g.lb
    targets = bf[...].reshape(g.kb * total, g.C).astype(BF16)
    scores = lax.dot_general(
        targets, a, (((1,), (1,)), ((), ())), preferred_element_type=F32
    ) * (g.C ** -0.5)
    volume = scores[:total]
    for kk in range(1, g.kb):
        volume = jnp.where(
            iota((total, LANES), 1) >= kk * g.ij, scores[kk * total : (kk + 1) * total], volume
        )
    vs[...] = volume.reshape(S, T * g.lb, LANES)

    @pl.loop(0, S)
    def _(ps):
        for tt in range(T):
            vp[ps + g.nl, tt + g.nk] = vs[ps, tt * g.lb : (tt + 1) * g.lb, :].astype(BF16)

    def block_to(n):
        other = lax.rem(me + n, N)
        os, ot = other // T, lax.rem(other, T)
        return pltpu.make_async_remote_copy(
            src_ref=vp.at[pl.ds(os, g.bl), pl.ds(ot, g.bk)], dst_ref=rb.at[s, t],
            send_sem=s_b.at[n], recv_sem=r_b.at[s, t],
            device_id={"src": os, "tgt": ot}, device_id_type=pl.DeviceIdType.MESH,
        )

    @pl.loop(1, N)
    def _(n):
        block_to(n).start()

    rb[s, t] = vp[pl.ds(s, g.bl), pl.ds(t, g.bk)]

    lane = iota((g.half, LANES), 1)
    wide = iota((g.kb * g.half, LANES), 1)

    def spread(ps):
        for tt in range(T):
            for dt in range(g.bk):
                for ds in range(g.bl):
                    at = dt * g.L + ds * g.lb
                    u[tt, at : at + g.lb, :] = rb[ps, tt, ds, dt].astype(F32)
        ins = [u[tt] for tt in range(T)]
        for ii in range(g.rows_i):
            parts = []
            for kk in range(g.kb):
                chunk = kk * g.rows_i + ii
                joined = None
                for tt in range(T):
                    shift = (tt - chunk) * g.cols_j % LANES
                    moved = pltpu.roll(ins[tt], shift, 1) if shift else ins[tt]
                    joined = moved if tt == 0 else jnp.where(lane >= tt * g.cols_j, moved, joined)
                parts.append(joined)
            x = jnp.concatenate(parts, axis=0)
            if g.KX > x.shape[0]:
                x = jnp.concatenate([x, jnp.zeros((g.KX - x.shape[0], LANES), F32)], axis=0)
            for sh in range(3):
                if sh == 0:
                    moved = jnp.where(iota(x.shape, 1) == 0, 0.0, pltpu.roll(x, 1, 1))
                elif sh == 2:
                    moved = jnp.where(
                        iota(x.shape, 1) == LANES - 1, 0.0, pltpu.roll(x, LANES - 1, 1)
                    )
                else:
                    moved = x
                moved = moved.astype(BF16)
                for r in range(3):
                    at = pl.multiple_of((ps * g.rows_i + (ii + 2 - r)) * LANES, LANES)
                    first = (r * 3 + sh) * g.KX
                    pat[first : first + g.KX, pl.ds(at, LANES)] = moved

    def arrive(ps, pt):
        pltpu.make_async_remote_copy(
            src_ref=rb.at[ps, pt], dst_ref=rb.at[ps, pt], send_sem=s_b.at[0],
            recv_sem=r_b.at[ps, pt], device_id={"src": ps, "tgt": pt},
            device_id_type=pl.DeviceIdType.MESH,
        ).wait_recv()

    @pl.loop(1, T)
    def _(m):
        arrive(s, lax.rem(t + m, T))

    spread(s)

    @pl.loop(1, S)
    def _(n):
        ps = lax.rem(s + n, S)

        @pl.loop(0, T)
        def _(m):
            arrive(ps, lax.rem(t + m, T))

        spread(ps)

    chunk = 4 * LANES

    @pl.loop(0, g.HA * LANES // chunk)
    def _(n):
        at = pl.multiple_of(LANES + n * chunk, LANES)
        patch = pat[:, pl.ds(at, chunk)]
        hid = jnp.maximum(dot(w1h[...], patch) + dot(w1l[...], patch), 0.0)
        hid_h, hid_l = split(hid)
        y[:, pl.ds(at, chunk)] = (
            dot(w2h[...], hid_h) + dot(w2l[...], hid_h) + dot(w2h[...], hid_l)
        )

    last = iota((g.unit, LANES), 1)
    for i in range(g.HA):
        sums = []
        for sh in range(3):
            part = None
            for r in range(3):
                first = (r * 3 + sh) * g.unit
                term = y[first : first + g.unit, (i + r) * LANES : (i + r + 1) * LANES]
                part = term if part is None else part + term
            sums.append(part)
        res = sums[1]
        res = res + jnp.where(last == 0, 0.0, pltpu.roll(sums[0], 1, 1))
        res = res + jnp.where(last == LANES - 1, 0.0, pltpu.roll(sums[2], LANES - 1, 1))
        for k in range(g.kb):
            for l in range(g.lb):
                n = k * g.lb + l
                out_ref[k, l, i : i + 1, :] = res[n : n + 1, :]

    @pl.loop(1, T)
    def _(m):
        to_column(m).wait_send()

    @pl.loop(0, T)
    def _(m):
        @pl.loop(1, S)
        def _(n):
            to_row(m, n).wait_send()

    @pl.loop(1, N)
    def _(n):
        block_to(n).wait_send()


def per_device(feature_a, feature_b, conv_in, bias_in, conv_out):
    S, T = lax.axis_size("src"), lax.axis_size("tgt")
    g = Plan(S, T, feature_a.shape, feature_b.shape, conv_in.shape[0])
    s1 = jnp.asarray(g.select_in(), BF16)
    s2 = jnp.asarray(g.select_out(), BF16)
    vm = pl.BlockSpec(memory_space=pltpu.VMEM)
    hbm = pl.BlockSpec(memory_space=pl.ANY)
    dma = pltpu.SemaphoreType.DMA
    return pl.pallas_call(
        functools.partial(kernel, g),
        out_shape=jax.ShapeDtypeStruct((g.kb, g.lb, g.HA, g.WA), F32),
        in_specs=[hbm, vm, vm, pl.BlockSpec(memory_space=pltpu.SMEM), vm, hbm, hbm],
        out_specs=vm,
        scratch_shapes=[
            pltpu.VMEM(feature_a.shape, BF16),
            pltpu.VMEM(s1.shape, BF16),
            pltpu.VMEM(s2.shape, BF16),
            dma((3,)),
            pltpu.VMEM((S, T, g.kb, g.lb, g.C), BF16),
            pltpu.VMEM((g.kb, S, T * g.lb, g.C), F32),
            pltpu.VMEM((S, T * g.lb, LANES), F32),
            pltpu.VMEM((S + 2 * g.nl, T + 2 * g.nk, g.lb, LANES), BF16),
            pltpu.VMEM((S, T, g.bl, g.bk, g.lb, LANES), BF16),
            pltpu.VMEM((T, g.half, LANES), F32),
            pltpu.VMEM((g.KP, (g.HA + 2) * LANES), BF16),
            pltpu.VMEM((g.M, g.KP), BF16),
            pltpu.VMEM((g.M, g.KP), BF16),
            pltpu.VMEM((g.Y, g.M), BF16),
            pltpu.VMEM((g.Y, g.M), BF16),
            pltpu.VMEM((g.Y, (g.HA + 2) * LANES), F32),
            pltpu.VMEM((g.hidden, LANES), F32),
            dma((T,)),
            dma((T, S)),
            dma((S, T)),
            dma((S * T,)),
            dma((S, T)),
        ],
        compiler_params=pltpu.CompilerParams(
            collective_id=0, has_side_effects=True, vmem_limit_bytes=44 * 1024 * 1024
        ),
    )(feature_a, feature_b, conv_in, bias_in, conv_out, s1, s2)


def solution(mesh):
    in_specs = (P("src", "tgt", None), P("tgt", "src", None), P(), P(), P())
    out_specs = P("tgt", "src", None, None)
    return jax.shard_map(
        per_device, mesh=mesh, in_specs=in_specs, out_specs=out_specs, check_vma=False
    )
```

time: 1890 us -> 34.1 us (0.02); the launches traced: 1860 us -> 33.6 us
  other arithmetic: 1670 us -> 0 us
  local copies, waits for them, and re-layouts: 127 us -> 6.51 us
  Pallas kernels: 0 us -> 27.1 us
  waiting for transfers between devices: 25 us -> 0 us
    mul x24 -> x0, other arithmetic: 849 us -> none  [the longest x16 425 us: channel_step(): jax.nn.relu(filter_taps(field, conv_in[channel_slot], extended) + bias_in...]
    add x8 -> x0, other arithmetic: 816 us -> none  [channel_step(): summed_total + filter_taps(jnp.pad(hidden_reflected, border_padding), ref...]
    slice x160 -> x0, local copies, waits for them, and re-layouts: 114 us -> none  [filter_taps(): weight = weights[first * 27 + second * 9 + third * 3 + fourth]]
    pallas_call x0 -> x1, Pallas kernels: none -> 27.1 us  [per_device(): pl.pallas_call(functools.partial(kernel, g), out_shape=jax.ShapeDtypeStru...]
    all_gather x1 -> x0, waiting for transfers between devices: 19.8 us -> none  [per_device(): piece = lax.all_gather(wide, 'src', axis=0, tiled=True)]
  transfers between devices with their start and end apart: 5 -> 0, of which waited for: 3 -> 0; matrix products, arithmetic and copies ran while one was open for 0% -> 0% of each run, Pallas kernels for 0% -> 0%
where the time goes in v1:
time: 34.1 us; the launch traced here: 33.6 us
  Pallas kernels  27.1 us (79%)
  local copies, waits for them, and re-layouts  6.51 us (19%)
    pallas_call x1, Pallas kernels, per_device(): pl.pallas_call(functools.partial(kernel, g), out_shape=jax.ShapeDtypeStru...  27.1 us
    unnamed x15, local copies, waits for them, and re-layouts  6.51 us

profile of v1, /device:TPU:1, one launch (start us, length us, event | category | flops | bytes accessed | tf_op | source)
XLA Modules:
  0.0 33.6 jit_solution(15204089467138140512)
XLA Ops:
  0.0 0.0 copy-start
  0.0 1.2 %copy-done = bf16[128,4096]{1,0:T(8,128)(2,1)S(1)} copy-done((bf16[128,4096]{1,0:T(8,128)(2,1)S(1)}, bf16[128,4096]{1,0:T(8,128)(2,1)}, u32[]{:S(2)}) %copy-start) | copy-done | bytes 1048600
  1.2 0.0 copy-start.1
  1.2 1.0 %copy-done.1 = bf16[128,2048]{1,0:T(8,128)(2,1)S(1)} copy-done((bf16[128,2048]{1,0:T(8,128)(2,1)S(1)}, bf16[128,2048]{1,0:T(8,128)(2,1)}, u32[]{:S(2)}) %copy-start.1) | copy-done | bytes 524312
  2.3 0.0 copy-start.2
  2.3 0.9 %copy-done.2 = bf16[2,32,1024]{2,1,0:T(8,128)(2,1)S(1)} copy-done((bf16[2,32,1024]{2,1,0:T(8,128)(2,1)S(1)}, bf16[2,32,1024]{2,1,0:T(8,128)(2,1)}, u32[]{:S(2)}) %copy-start.2) | copy-done | bytes 131096
  3.2 0.0 copy-start.3
  3.2 0.7 %copy-done.3 = bf16[2,2,1024]{2,1,0:T(2,128)(2,1)S(1)} copy-done((bf16[2,2,1024]{2,1,0:T(2,128)(2,1)S(1)}, bf16[2,2,1024]{2,1,0:T(2,128)(2,1)}, u32[]{:S(2)}) %copy-start.3) | copy-done | bytes 8216
  3.9 0.0 copy-start.4
  3.9 0.7 %copy-done.4 = f32[8,81]{1,0:T(8,128)S(1)} copy-done((f32[8,81]{1,0:T(8,128)S(1)}, f32[8,81]{1,0:T(8,128)}, u32[]{:S(2)}) %copy-start.4) | copy-done | bytes 2616
  4.6 0.0 copy-start.5
  4.6 0.7 %copy-done.5 = f32[8,81]{1,0:T(8,128)S(1)} copy-done((f32[8,81]{1,0:T(8,128)S(1)}, f32[8,81]{1,0:T(8,128)}, u32[]{:S(2)}) %copy-start.5) | copy-done | bytes 2616
  5.2 0.0 copy-start.6
  5.2 0.7 %copy-done.6 = f32[8]{0:T(128)S(1)} copy-done((f32[8]{0:T(128)S(1)}, f32[8]{0:T(128)}, u32[]{:S(2)}) %copy-start.6) | copy-done | bytes 56
  5.9 27.1 %shard_map.73 = f32[2,2,16,128]{3,2,1,0:T(8,128)S(1)} custom-call(bf16[2,32,1024]{2,1,0:T(8,128)(2,1)S(1)} %copy-done.2, bf16[2,2,1024]{2,1,0:T(2,128)(2,1)S(1)} %copy-done.3, f32[8,81]{1,0:T(8,128)S(1)} %copy-done.4, f32[8]{0:T(128)S(1)} %copy-done.6, f32[8,81]{1,0:T(8,128)S(1)} %copy-done.5, bf16[128,2048]{1,0:T(8,128)(2,1)S(1)} %copy-done.1, ...), custom_call_target="tpu_custom_call" | custom-call | tf_op jit(solution)/shard_map/pallas_call | solution.py:368
  33.0 0.6 %copy.9 = f32[2,2,16,128]{3,2,1,0:T(8,128)} copy(f32[2,2,16,128]{3,2,1,0:T(8,128)S(1)} %shard_map.73) | data formatting | bytes 65536
Async XLA Ops:
  0.0 1.2 %copy-start = (bf16[128,4096]{1,0:T(8,128)(2,1)S(1)}, bf16[128,4096]{1,0:T(8,128)(2,1)}, u32[]{:S(2)}) copy-start(bf16[128,4096]{1,0:T(8,128)(2,1)} %constant.5.clone.s2_hbm) | copy-start | bytes 3145732
  1.2 1.0 %copy-start.1 = (bf16[128,2048]{1,0:T(8,128)(2,1)S(1)}, bf16[128,2048]{1,0:T(8,128)(2,1)}, u32[]{:S(2)}) copy-start(bf16[128,2048]{1,0:T(8,128)(2,1)} %constant.4.clone.s1_hbm) | copy-start | bytes 1572868
  2.3 0.9 %copy-start.2 = (bf16[2,32,1024]{2,1,0:T(8,128)(2,1)S(1)}, bf16[2,32,1024]{2,1,0:T(8,128)(2,1)}, u32[]{:S(2)}) copy-start(bf16[2,32,1024]{2,1,0:T(8,128)(2,1)} %a_hbm.1) | copy-start | bytes 393220
  3.2 0.7 %copy-start.3 = (bf16[2,2,1024]{2,1,0:T(2,128)(2,1)S(1)}, bf16[2,2,1024]{2,1,0:T(2,128)(2,1)}, u32[]{:S(2)}) copy-start(bf16[2,2,1024]{2,1,0:T(2,128)(2,1)} %b_ref.1) | copy-start | bytes 24580
  3.9 0.7 %copy-start.4 = (f32[8,81]{1,0:T(8,128)S(1)}, f32[8,81]{1,0:T(8,128)}, u32[]{:S(2)}) copy-start(f32[8,81]{1,0:T(8,128)} %cin_ref.1) | copy-start | bytes 7780
  4.6 0.7 %copy-start.5 = (f32[8,81]{1,0:T(8,128)S(1)}, f32[8,81]{1,0:T(8,128)}, u32[]{:S(2)}) copy-start(f32[8,81]{1,0:T(8,128)} %cout_ref.1) | copy-start | bytes 7780
  5.2 0.7 %copy-start.6 = (f32[8]{0:T(128)S(1)}, f32[8]{0:T(128)}, u32[]{:S(2)}) copy-start(f32[8]{0:T(128)} %bias_ref.1) | copy-start | bytes 100

commit v2 on v1

--- a/solution.py
+++ b/solution.py
@@ -81,9 +81,10 @@
 
 
 def kernel(
-    g, a_hbm, b_ref, cin_ref, bias_ref, cout_ref, s1_hbm, s2_hbm, out_ref,
-    a_vm, s1_vm, s2_vm, load_sem, bb, bf, vs, vp, rb, u, pat, w1h, w1l, w2h, w2l, y, cpad,
-    s_a1, s_a2, r_a, s_b, r_b,
+    g, a_hbm, b_hbm, cin_hbm, bias_hbm, cout_hbm, s1_hbm, s2_hbm, out_ref,
+    a_vm, b_ref, cin_ref, bias_ref, cout_ref, s1_vm, s2_vm, load_sem,
+    bb, bf, vs, vp, rb, u, pat, w1h, w1l, w2h, w2l, y, cpad,
+    s_a1, s_a2, r_a1, r_a2, s_b1, s_b2, r_b,
 ):
     S, T = g.S, g.T
     N = S * T
@@ -92,57 +93,54 @@
     me = s * T + t
 
     loads = [
-        pltpu.make_async_copy(a_hbm, a_vm, load_sem.at[0]),
-        pltpu.make_async_copy(s1_hbm, s1_vm, load_sem.at[1]),
-        pltpu.make_async_copy(s2_hbm, s2_vm, load_sem.at[2]),
+        pltpu.make_async_copy(src, dst, load_sem.at[n])
+        for n, (src, dst) in enumerate((
+            (b_hbm, b_ref), (cin_hbm, cin_ref), (bias_hbm, bias_ref), (s1_hbm, s1_vm),
+            (cout_hbm, cout_ref), (s2_hbm, s2_vm), (a_hbm, a_vm),
+        ))
     ]
     for load in loads:
         load.start()
 
     barrier = pltpu.get_barrier_semaphore()
 
-    @pl.loop(1, N)
-    def _(n):
-        other = lax.rem(me + n, N)
+    def greet(ps, pt):
         pl.semaphore_signal(
-            barrier, inc=1, device_id={"src": other // T, "tgt": lax.rem(other, T)},
-            device_id_type=pl.DeviceIdType.MESH,
-        )
-
+            barrier, inc=1, device_id={"src": ps, "tgt": pt}, device_id_type=pl.DeviceIdType.MESH
+        )
+
+    for m in range(1, T):
+        greet(s, lax.rem(t + m, T))
+    for n in range(1, S):
+        greet(lax.rem(s + n, S), t)
+    loads[0].wait()
     bb[s, t] = b_ref[...]
     vp[...] = jnp.zeros(vp.shape, BF16)
-    pl.semaphore_wait(barrier, N - 1)
-
-    def piece(ps, pt, send, ds, dt):
+    pl.semaphore_wait(barrier, S + T - 2)
+
+    def piece(pt, send, recv, ds, dt):
         return pltpu.make_async_remote_copy(
-            src_ref=bb.at[ps, pt], dst_ref=bb.at[ps, pt], send_sem=send,
-            recv_sem=r_a.at[ps, pt], device_id={"src": ds, "tgt": dt},
-            device_id_type=pl.DeviceIdType.MESH,
-        )
-
-    def to_row(m, n):
-        return piece(s, lax.rem(t + m, T), s_a2.at[m, n], lax.rem(s + n, S), t)
-
-    def to_column(m):
-        return piece(s, t, s_a1.at[m], s, lax.rem(t + m, T))
-
-    @pl.loop(1, T)
-    def _(m):
-        to_column(m).start()
-
-    @pl.loop(1, S)
-    def _(n):
-        to_row(0, n).start()
-
-    @pl.loop(1, T)
-    def _(m):
-        piece(s, lax.rem(t + m, T), s_a1.at[m], s, lax.rem(t + m, T)).wait_recv()
-
-        @pl.loop(1, S)
-        def _(n):
-            to_row(m, n).start()
-
-    loads[1].wait()
+            src_ref=bb.at[s, pt], dst_ref=bb.at[s, pt], send_sem=send, recv_sem=recv,
+            device_id={"src": ds, "tgt": dt}, device_id_type=pl.DeviceIdType.MESH,
+        )
+
+    def taken(ref, sem):
+        pltpu.make_async_copy(ref, ref, sem).wait()
+
+    def to_row(pt):
+        for n in range(1, S):
+            piece(pt, s_a2.at[0], r_a2.at[s], lax.rem(s + n, S), t).start()
+
+    for m in range(1, T):
+        piece(t, s_a1.at[0], r_a1.at[t], s, lax.rem(t + m, T)).start()
+    to_row(t)
+    for m in range(1, T):
+        pt = lax.rem(t + m, T)
+        taken(bb.at[s, pt], r_a1.at[pt])
+        to_row(pt)
+
+    for load in loads[1:4]:
+        load.wait()
     cpad[...] = jnp.zeros(cpad.shape, F32)
     cpad[:, : cin_ref.shape[1]] = cin_ref[...]
     taps_h, taps_l = split(cpad[...])
@@ -176,7 +174,8 @@
             w1h[at : at + 2 * H, :] = block[: 2 * H, : g.KP].astype(BF16)
             w1l[at : at + 2 * H, :] = block[2 * H :, : g.KP].astype(BF16)
 
-    loads[2].wait()
+    loads[4].wait()
+    loads[5].wait()
     cpad[:, : cout_ref.shape[1]] = cout_ref[...]
     taps_h, taps_l = split(cpad[...])
     both = jnp.concatenate([taps_h.astype(F32), taps_l.astype(F32)], axis=0).astype(BF16)
@@ -197,7 +196,7 @@
     y[:, :LANES] = jnp.zeros((g.Y, LANES), F32)
     y[:, (g.HA + 1) * LANES :] = jnp.zeros((g.Y, LANES), F32)
 
-    loads[0].wait()
+    loads[6].wait()
     a = a_vm[...].astype(F32).reshape(g.ij, g.C)
     a = jnp.concatenate([a] * (LANES // g.ij), axis=0).astype(BF16)
 
@@ -208,15 +207,9 @@
 
     take(s)
 
-    @pl.loop(1, S)
-    def _(n):
+    for n in range(1, S):
         ps = lax.rem(s + n, S)
-
-        @pl.loop(0, T)
-        def _(m):
-            pt = lax.rem(t + m, T)
-            piece(ps, pt, s_a2.at[m, n], ps, t).wait_recv()
-
+        taken(bb.at[ps], r_a2.at[ps])
         take(ps)
 
     total = S * T * g.lb
@@ -231,25 +224,29 @@
         )
     vs[...] = volume.reshape(S, T * g.lb, LANES)
 
-    @pl.loop(0, S)
-    def _(ps):
+    for ps in range(S):
         for tt in range(T):
             vp[ps + g.nl, tt + g.nk] = vs[ps, tt * g.lb : (tt + 1) * g.lb, :].astype(BF16)
 
-    def block_to(n):
-        other = lax.rem(me + n, N)
-        os, ot = other // T, lax.rem(other, T)
-        return pltpu.make_async_remote_copy(
-            src_ref=vp.at[pl.ds(os, g.bl), pl.ds(ot, g.bk)], dst_ref=rb.at[s, t],
-            send_sem=s_b.at[n], recv_sem=r_b.at[s, t],
-            device_id={"src": os, "tgt": ot}, device_id_type=pl.DeviceIdType.MESH,
-        )
-
-    @pl.loop(1, N)
-    def _(n):
-        block_to(n).start()
-
-    rb[s, t] = vp[pl.ds(s, g.bl), pl.ds(t, g.bk)]
+    def block_to(ps, pt, send):
+        pltpu.make_async_remote_copy(
+            src_ref=vp.at[pl.ds(ps, g.bl), pl.ds(pt, g.bk)], dst_ref=rb.at[s, t],
+            send_sem=send, recv_sem=r_b.at[s],
+            device_id={"src": ps, "tgt": pt}, device_id_type=pl.DeviceIdType.MESH,
+        ).start()
+
+    for m in range(T - 1, -1, -1):
+        pt = lax.rem(t + m, T)
+        for n in range(S):
+            if n:
+                block_to(lax.rem(s + n, S), pt, s_b2.at[0])
+            elif m:
+                block_to(s, pt, s_b1.at[0])
+    pltpu.make_async_copy(
+        vp.at[pl.ds(s, g.bl), pl.ds(t, g.bk)], rb.at[s, t], r_b.at[s]
+    ).start()
+    taken(bb.at[0, : T - 1], s_a1.at[0])
+    taken(bb.at[: S - 1], s_a2.at[0])
 
     lane = iota((g.half, LANES), 1)
     wide = iota((g.kb * g.half, LANES), 1)
@@ -285,44 +282,29 @@
                     moved = x
                 moved = moved.astype(BF16)
                 for r in range(3):
-                    at = pl.multiple_of((ps * g.rows_i + (ii + 2 - r)) * LANES, LANES)
+                    at = (ps * g.rows_i + (ii + 2 - r)) * LANES
                     first = (r * 3 + sh) * g.KX
-                    pat[first : first + g.KX, pl.ds(at, LANES)] = moved
-
-    def arrive(ps, pt):
-        pltpu.make_async_remote_copy(
-            src_ref=rb.at[ps, pt], dst_ref=rb.at[ps, pt], send_sem=s_b.at[0],
-            recv_sem=r_b.at[ps, pt], device_id={"src": ps, "tgt": pt},
-            device_id_type=pl.DeviceIdType.MESH,
-        ).wait_recv()
-
-    @pl.loop(1, T)
-    def _(m):
-        arrive(s, lax.rem(t + m, T))
-
-    spread(s)
-
-    @pl.loop(1, S)
-    def _(n):
-        ps = lax.rem(s + n, S)
-
-        @pl.loop(0, T)
-        def _(m):
-            arrive(ps, lax.rem(t + m, T))
-
-        spread(ps)
-
-    chunk = 4 * LANES
-
-    @pl.loop(0, g.HA * LANES // chunk)
-    def _(n):
-        at = pl.multiple_of(LANES + n * chunk, LANES)
-        patch = pat[:, pl.ds(at, chunk)]
+                    pat[first : first + g.KX, at : at + LANES] = moved
+
+    def filters(ps):
+        at, chunk = (1 + ps * g.rows_i) * LANES, g.rows_i * LANES
+        patch = pat[:, at : at + chunk]
         hid = jnp.maximum(dot(w1h[...], patch) + dot(w1l[...], patch), 0.0)
         hid_h, hid_l = split(hid)
-        y[:, pl.ds(at, chunk)] = (
+        y[:, at : at + chunk] = (
             dot(w2h[...], hid_h) + dot(w2l[...], hid_h) + dot(w2h[...], hid_l)
         )
+
+    for ps in range(S):
+        taken(rb.at[ps], r_b.at[ps])
+        if ps == 1:
+            taken(rb.at[0, : T - 1], s_b1.at[0])
+            taken(rb.at[: S - 1], s_b2.at[0])
+        spread(ps)
+        if ps >= 2:
+            filters(ps - 2)
+    for ps in range(max(S - 2, 0), S):
+        filters(ps)
 
     last = iota((g.unit, LANES), 1)
     for i in range(g.HA):
@@ -342,20 +324,6 @@
                 n = k * g.lb + l
                 out_ref[k, l, i : i + 1, :] = res[n : n + 1, :]
 
-    @pl.loop(1, T)
-    def _(m):
-        to_column(m).wait_send()
-
-    @pl.loop(0, T)
-    def _(m):
-        @pl.loop(1, S)
-        def _(n):
-            to_row(m, n).wait_send()
-
-    @pl.loop(1, N)
-    def _(n):
-        block_to(n).wait_send()
-
 
 def per_device(feature_a, feature_b, conv_in, bias_in, conv_out):
     S, T = lax.axis_size("src"), lax.axis_size("tgt")
@@ -368,13 +336,17 @@
     return pl.pallas_call(
         functools.partial(kernel, g),
         out_shape=jax.ShapeDtypeStruct((g.kb, g.lb, g.HA, g.WA), F32),
-        in_specs=[hbm, vm, vm, pl.BlockSpec(memory_space=pltpu.SMEM), vm, hbm, hbm],
+        in_specs=[hbm] * 7,
         out_specs=vm,
         scratch_shapes=[
             pltpu.VMEM(feature_a.shape, BF16),
+            pltpu.VMEM(feature_b.shape, BF16),
+            pltpu.VMEM(conv_in.shape, F32),
+            pltpu.SMEM(bias_in.shape, F32),
+            pltpu.VMEM(conv_out.shape, F32),
             pltpu.VMEM(s1.shape, BF16),
             pltpu.VMEM(s2.shape, BF16),
-            dma((3,)),
+            dma((7,)),
             pltpu.VMEM((S, T, g.kb, g.lb, g.C), BF16),
             pltpu.VMEM((g.kb, S, T * g.lb, g.C), F32),
             pltpu.VMEM((S, T * g.lb, LANES), F32),
@@ -388,14 +360,16 @@
             pltpu.VMEM((g.Y, g.M), BF16),
             pltpu.VMEM((g.Y, (g.HA + 2) * LANES), F32),
             pltpu.VMEM((g.hidden, LANES), F32),
+            dma((1,)),
+            dma((1,)),
             dma((T,)),
-            dma((T, S)),
-            dma((S, T)),
-            dma((S * T,)),
-            dma((S, T)),
+            dma((S,)),
+            dma((1,)),
+            dma((1,)),
+            dma((S,)),
         ],
         compiler_params=pltpu.CompilerParams(
-            collective_id=0, has_side_effects=True, vmem_limit_bytes=44 * 1024 * 1024
+            collective_id=0, has_side_effects=True, vmem_limit_bytes=62 * 1024 * 1024
         ),
     )(feature_a, feature_b, conv_in, bias_in, conv_out, s1, s2)
 

time: 34.1 us -> 26.6 us (0.78)
  local copies, waits for them, and re-layouts: 6.51 us -> 1.38 us
  Pallas kernels: 27.1 us -> 24.6 us
    unnamed x15 -> x1, local copies, waits for them, and re-layouts: 6.51 us -> 1.38 us
    pallas_call x1, Pallas kernels: 27.1 us -> 24.6 us  [per_device(): pl.pallas_call(functools.partial(kernel, g), out_shape=jax.ShapeDtypeStru...]
where the time goes in v2:
time: 26.6 us; the launch traced here: 26 us
  Pallas kernels  24.6 us (92%)
  local copies, waits for them, and re-layouts  1.38 us (5%)
    pallas_call x1, Pallas kernels, per_device(): pl.pallas_call(functools.partial(kernel, g), out_shape=jax.ShapeDtypeStru...  24.6 us
    unnamed x1, local copies, waits for them, and re-layouts  1.38 us

profile of v2, /device:TPU:1, one launch (start us, length us, event | category | flops | bytes accessed | tf_op | source)
XLA Modules:
  0.0 26.0 jit_solution(14045026261140975451)
XLA Ops:
  0.0 24.6 %shard_map.73 = f32[2,2,16,128]{3,2,1,0:T(8,128)} custom-call(bf16[2,32,1024]{2,1,0:T(8,128)(2,1)} %a_hbm.1, bf16[2,2,1024]{2,1,0:T(2,128)(2,1)} %b_hbm.1, f32[8,81]{1,0:T(8,128)} %cin_hbm.1, f32[8]{0:T(128)} %bias_hbm.1, f32[8,81]{1,0:T(8,128)} %cout_hbm.1, bf16[128,2048]{1,0:T(8,128)(2,1)} %constant.4.clone.s1_hbm, bf16[128,4096]{1,0:T(8,128)(2,1)} %constant.5.clone.s2_hbm), custom_call_target="tpu_custom_call" | custom-call | tf_op jit(solution)/shard_map/pallas_call | solution.py:336
  24.6 1.4 %copy.9 = f32[2,2,16,128]{3,2,1,0:T(8,128)} copy(f32[2,2,16,128]{3,2,1,0:T(8,128)} %shard_map.73) | data formatting | bytes 65536

commit v3 on v2

v3 whole, which is shorter than its diff:
```python
import functools

import jax
import jax.numpy as jnp
import numpy as np
from jax import lax
from jax.experimental import pallas as pl
from jax.experimental.pallas import tpu as pltpu
from jax.sharding import PartitionSpec as P

LANES = 128
F32 = jnp.float32
BF16 = jnp.bfloat16


def round_up(value, unit):
    return -(-value // unit) * unit


class Plan:
    def __init__(self, count_s, count_t, a_shape, b_shape, hidden):
        self.S, self.T = count_s, count_t
        self.rows_i, self.cols_j, self.C = a_shape
        self.kb, self.lb = b_shape[0], b_shape[1]
        self.hidden = hidden
        self.G = 2
        assert count_s % self.G == 0
        self.H2 = count_s // self.G
        self.ij = self.rows_i * self.cols_j
        self.HA = self.rows_i * count_s
        self.WA = self.cols_j * count_t
        self.pair = self.G * self.ij
        assert self.WA == LANES and LANES % self.pair == 0 and self.kb >= 2 and self.lb >= 2
        self.bk = self.bl = 3
        self.block = self.kb * self.lb
        self.used = self.bk * self.bl * self.block
        self.rows = round_up(self.used + 1, 8)
        self.KX = round_up(self.rows, 16)
        self.KP = 9 * self.KX
        self.KW = round_up(self.KP, LANES)
        self.hk, self.hl = self.kb + 2, self.lb + 2
        self.M = self.hk * self.hl * 2 * hidden
        self.unit = round_up(self.block, 8)
        self.Y = round_up(9 * self.unit, 16)
        assert self.Y <= LANES

    def tap(self, net, p, q, r, s):
        p, q, r, s = (p, q, r, s) if net == 0 else (r, s, p, q)
        return 27 * p + 9 * q + 3 * r + s

    def select_in(self):
        out = np.zeros((LANES, self.kb, self.lb, 2, self.KW), np.float32)
        for k, l, net in np.ndindex(self.kb, self.lb, 2):
            for p, q, r, s in np.ndindex(3, 3, 3, 3):
                ek, el = k + p - 2 + self.kb, l + q - 2 + self.lb
                col = (r * 3 + s) * self.KX + (el % self.lb) + (ek % self.kb) * self.lb
                col += (el // self.lb * self.bk + ek // self.kb) * self.block
                out[self.tap(net, p, q, r, s), k, l, net, col] = 1
        return out.reshape(LANES, -1)

    def select_out(self):
        out = np.zeros((LANES, self.hk, self.hl, 2, LANES), np.float32)
        for k, l, net in np.ndindex(self.hk, self.hl, 2):
            for ok, ol, r, s in np.ndindex(self.kb, self.lb, 3, 3):
                p, q = k - ok, l - ol
                if 0 <= p < 3 and 0 <= q < 3:
                    col = (r * 3 + s) * self.unit + ok * self.lb + ol
                    out[self.tap(net, p, q, r, s), k, l, net, col] = 1
        return out.reshape(LANES, -1)


def split(x):
    high = x.astype(BF16)
    return high, (x - high.astype(F32)).astype(BF16)


def dot(x, y):
    return jnp.dot(x, y, preferred_element_type=F32)


def iota(shape, dim):
    return lax.broadcasted_iota(jnp.int32, shape, dim)


def kernel(
    g, a_hbm, b_hbm, cin_hbm, bias_hbm, cout_hbm, s1_hbm, s2_hbm, out_ref,
    ach, b_ref, cin_ref, bias_ref, cout_ref, s1_vm, s2_vm, load_sem,
    bb, bf, vs, vp, r1, r2, u, pat, w1h, w1l, w2h, w2l, y, cpad,
    s_x, r_x, s_a, r_a, s_b1, s_b2, r_b1, r_b2,
):
    S, T = g.S, g.T
    H2 = g.H2
    N = H2 * T
    s = lax.axis_index("src")
    t = lax.axis_index("tgt")
    core = lax.rem(s, g.G)
    h = s // g.G
    sibling = s + 1 - 2 * core

    loads = [
        pltpu.make_async_copy(src, dst, load_sem.at[n])
        for n, (src, dst) in enumerate((
            (b_hbm, b_ref), (cin_hbm, cin_ref), (bias_hbm, bias_ref), (s1_hbm, s1_vm),
            (cout_hbm, cout_ref), (s2_hbm, s2_vm), (a_hbm, ach.at[core]),
        ))
    ]
    for load in loads:
        load.start()

    barrier = pltpu.get_barrier_semaphore()

    def greet(ps, pt):
        pl.semaphore_signal(
            barrier, inc=1, device_id={"src": ps, "tgt": pt}, device_id_type=pl.DeviceIdType.MESH
        )

    peers = [
        (lax.rem(h + n, H2), lax.rem(t + m, T)) for n in range(H2) for m in range(T) if n or m
    ]
    greet(sibling, t)
    for ph, pt in peers:
        greet(ph * g.G + core, pt)
    loads[0].wait()
    vp[...] = jnp.zeros(vp.shape, BF16)
    pl.semaphore_wait(barrier, N)

    def remote(src, dst, send, recv, ps, pt):
        return pltpu.make_async_remote_copy(
            src_ref=src, dst_ref=dst, send_sem=send, recv_sem=recv,
            device_id={"src": ps, "tgt": pt}, device_id_type=pl.DeviceIdType.MESH,
        )

    def taken(ref, sem):
        pltpu.make_async_copy(ref, ref, sem).wait()

    for ph, pt in peers:
        remote(b_ref, bb.at[h, t], s_a.at[0], r_a.at[h], ph * g.G + core, pt).start()
    swap = remote(a_hbm, ach.at[core], s_x.at[0], r_x.at[0], sibling, t)
    swap.start()
    pltpu.make_async_copy(b_ref, bb.at[h, t], r_a.at[h]).start()

    for load in loads[1:4]:
        load.wait()
    cpad[...] = jnp.zeros(cpad.shape, F32)
    cpad[:, : cin_ref.shape[1]] = cin_ref[...]
    taps_h, taps_l = split(cpad[...])
    both = jnp.concatenate([taps_h.astype(F32), taps_l.astype(F32)], axis=0).astype(BF16)
    base = dot(both, s1_vm[...])
    H = g.hidden
    row = iota((H, LANES), 0)
    bias = jnp.zeros((H, LANES), F32)
    for n in range(H):
        bias = jnp.where(row == n, bias_ref[n], bias)
    bias_h, bias_l = (part.astype(F32) for part in split(bias))
    bias = jnp.concatenate([bias_h, bias_h, bias_l, bias_l], axis=0)
    bias = jnp.concatenate([bias] * (g.KW // LANES), axis=1)
    bias = jnp.where(iota(bias.shape, 1) == 4 * g.KX + g.rows - 1, bias, 0.0)
    for k in range(g.hk):
        at_k = t * g.kb + (k - 1)
        for l in range(g.hl):
            at_l = s * g.lb + (l - 1)
            parts = []
            for first in (0, H):
                for net in range(2):
                    at = ((k % g.kb * g.lb + l % g.lb) * 2 + net) * g.KW
                    parts.append(base[first : first + H, at : at + g.KW])
            block = jnp.concatenate(parts, axis=0)
            shift = (l // g.lb * g.bk + k // g.kb) * g.block
            if shift:
                block = pltpu.roll(block, shift, 1)
            inside = (at_k >= 0) & (at_k < T * g.kb) & (at_l >= 0) & (at_l < S * g.lb)
            block = (block + bias) * jnp.where(inside, 1.0, 0.0).astype(F32)
            at = (k * g.hl + l) * 2 * H
            w1h[at : at + 2 * H, :] = block[: 2 * H, : g.KP].astype(BF16)
            w1l[at : at + 2 * H, :] = block[2 * H :, : g.KP].astype(BF16)

    loads[4].wait()
    loads[5].wait()
    cpad[:, : cout_ref.shape[1]] = cout_ref[...]
    taps_h, taps_l = split(cpad[...])
    both = jnp.concatenate([taps_h.astype(F32), taps_l.astype(F32)], axis=0).astype(BF16)
    base = dot(both, s2_vm[...])
    blocks = g.hk * g.hl * 2
    for first, ref in ((0, w2h), (H, w2l)):
        tall = jnp.concatenate(
            [base[first : first + H, n * LANES : (n + 1) * LANES] for n in range(blocks)], axis=0
        )
        ref[...] = tall.T[: g.Y].astype(BF16)

    tail = g.rows - g.used
    u[:, :, g.used :, :] = jnp.where(
        iota((H2, T, tail, LANES), 2) == tail - 1, jnp.ones((H2, T, tail, LANES), F32), 0.0
    )
    pat[: 3 * g.KX, LANES : 2 * LANES] = jnp.zeros((3 * g.KX, LANES), BF16)
    pat[6 * g.KX :, g.HA * LANES : (g.HA + 1) * LANES] = jnp.zeros((3 * g.KX, LANES), BF16)
    y[:, :LANES] = jnp.zeros((g.Y, LANES), F32)
    y[:, (g.HA + 1) * LANES :] = jnp.zeros((g.Y, LANES), F32)

    loads[6].wait()
    swap.wait_recv()
    a = ach[...].astype(F32).reshape(g.pair, g.C)
    a = jnp.concatenate([a] * (LANES // g.pair), axis=0).astype(BF16)

    for n in range(H2):
        ph = lax.rem(h + n, H2)
        taken(bb.at[ph], r_a.at[ph])
        for tt in range(T):
            for kk in range(g.kb):
                at = tt * g.block + kk * g.lb
                bf[ph, at : at + g.lb, :] = bb[ph, tt, kk].astype(F32)

    total = N * g.block
    targets = bf[...].reshape(total, g.C).astype(BF16)
    volume = lax.dot_general(
        targets, a, (((1,), (1,)), ((), ())), preferred_element_type=F32
    ) * (g.C ** -0.5)
    vs[...] = volume.reshape(H2, T * g.block, LANES)
    for ph in range(H2):
        for tt in range(T):
            vp[ph + 1, tt + 1] = vs[ph, tt * g.block : (tt + 1) * g.block, :].astype(BF16)

    def near(ph, pt):
        return vp.at[pl.ds(ph + 1, 1), pl.ds(pt, g.bk)]

    def other(ph, pt):
        return vp.at[pl.ds(ph + 1 - core, 2), pl.ds(pt, g.bk)]

    for ph, pt in peers + [(h, t)]:
        remote(
            other(ph, pt), r2.at[h, t], s_b2.at[0], r_b2.at[h], ph * g.G + 1 - core, pt
        ).start()
    for ph, pt in peers:
        remote(near(ph, pt), r1.at[h, t], s_b1.at[0], r_b1.at[h], ph * g.G + core, pt).start()
    pltpu.make_async_copy(near(h, t), r1.at[h, t], r_b1.at[h]).start()
    for ph, pt in peers:
        pltpu.make_async_copy(b_ref, b_ref, s_a.at[0]).wait()
    swap.wait_send()

    lane = iota((g.rows, LANES), 1)
    wide = iota((g.KX, LANES), 1)
    rows_h = g.G * g.rows_i

    def spread(ph):
        ins = []
        for tt in range(T):
            for dt in range(g.bk):
                for ds in range(g.bl):
                    at = (ds * g.bk + dt) * g.block
                    got = r1[ph, tt, 0, dt] if ds == 1 else r2[ph, tt, ds // 2, dt]
                    u[ph, tt, at : at + g.block, :] = got.astype(F32)
            ins.append(u[ph, tt])
        for chunk in range(rows_h):
            x = None
            for tt in range(T):
                shift = (tt - chunk) * g.cols_j % LANES
                moved = pltpu.roll(ins[tt], shift, 1) if shift else ins[tt]
                x = moved if tt == 0 else jnp.where(lane >= tt * g.cols_j, moved, x)
            if g.KX > g.rows:
                x = jnp.concatenate([x, jnp.zeros((g.KX - g.rows, LANES), F32)], axis=0)
            for sh in range(3):
                if sh == 0:
                    moved = jnp.where(wide == 0, 0.0, pltpu.roll(x, 1, 1))
                elif sh == 2:
                    moved = jnp.where(wide == LANES - 1, 0.0, pltpu.roll(x, LANES - 1, 1))
                else:
                    moved = x
                moved = moved.astype(BF16)
                for r in range(3):
                    at = (ph * rows_h + chunk + 2 - r) * LANES
                    first = (r * 3 + sh) * g.KX
                    pat[first : first + g.KX, at : at + LANES] = moved

    def filters(n):
        at = LANES + n * wide_n
        patch = pat[:, at : at + wide_n]
        hid = jnp.maximum(dot(w1h[...], patch) + dot(w1l[...], patch), 0.0)
        hid_h, hid_l = split(hid)
        y[:, at : at + wide_n] = (
            dot(w2h[...], hid_h) + dot(w2l[...], hid_h) + dot(w2h[...], hid_l)
        )

    for ph in range(H2):
        taken(r1.at[ph], r_b1.at[ph])
        taken(r2.at[ph], r_b2.at[ph])
    wide_n = 2 * LANES
    done = 0
    for ph in range(H2):
        spread(ph)
        ready = g.HA if ph == H2 - 1 else (ph + 1) * rows_h - 1
        while (done + 1) * wide_n <= ready * LANES:
            filters(done)
            done += 1

    last = iota((g.unit, LANES), 1)
    for i in range(g.HA):
        sums = []
        for sh in range(3):
            part = None
            for r in range(3):
                first = (r * 3 + sh) * g.unit
                term = y[first : first + g.unit, (i + r) * LANES : (i + r + 1) * LANES]
                part = term if part is None else part + term
            sums.append(part)
        res = sums[1]
        res = res + jnp.where(last == 0, 0.0, pltpu.roll(sums[0], 1, 1))
        res = res + jnp.where(last == LANES - 1, 0.0, pltpu.roll(sums[2], LANES - 1, 1))
        for k in range(g.kb):
            for l in range(g.lb):
                n = k * g.lb + l
                out_ref[k, l, i : i + 1, :] = res[n : n + 1, :]

    taken(r2, s_b2.at[0])
    for ph, pt in peers:
        pltpu.make_async_copy(r1.at[0, 0], r1.at[0, 0], s_b1.at[0]).wait()


def per_device(feature_a, feature_b, conv_in, bias_in, conv_out):
    S, T = lax.axis_size("src"), lax.axis_size("tgt")
    g = Plan(S, T, feature_a.shape, feature_b.shape, conv_in.shape[0])
    s1 = jnp.asarray(g.select_in(), BF16)
    s2 = jnp.asarray(g.select_out(), BF16)
    vm = pl.BlockSpec(memory_space=pltpu.VMEM)
    hbm = pl.BlockSpec(memory_space=pl.ANY)
    dma = pltpu.SemaphoreType.DMA
    return pl.pallas_call(
        functools.partial(kernel, g),
        out_shape=jax.ShapeDtypeStruct((g.kb, g.lb, g.HA, g.WA), F32),
        in_specs=[hbm] * 7,
        out_specs=vm,
        scratch_shapes=[
            pltpu.VMEM((g.G,) + feature_a.shape, BF16),
            pltpu.VMEM(feature_b.shape, BF16),
            pltpu.VMEM(conv_in.shape, F32),
            pltpu.SMEM(bias_in.shape, F32),
            pltpu.VMEM(conv_out.shape, F32),
            pltpu.VMEM(s1.shape, BF16),
            pltpu.VMEM(s2.shape, BF16),
            dma((7,)),
            pltpu.VMEM((g.H2, T, g.kb, g.lb, g.C), BF16),
            pltpu.VMEM((g.H2, T * g.block, g.C), F32),
            pltpu.VMEM((g.H2, T * g.block, LANES), F32),
            pltpu.VMEM((g.H2 + 2, T + 2, g.block, LANES), BF16),
            pltpu.VMEM((g.H2, T, 1, g.bk, g.block, LANES), BF16),
            pltpu.VMEM((g.H2, T, 2, g.bk, g.block, LANES), BF16),
            pltpu.VMEM((g.H2, T, g.rows, LANES), F32),
            pltpu.VMEM((g.KP, (g.HA + 2) * LANES), BF16),
            pltpu.VMEM((g.M, g.KP), BF16),
            pltpu.VMEM((g.M, g.KP), BF16),
            pltpu.VMEM((g.Y, g.M), BF16),
            pltpu.VMEM((g.Y, g.M), BF16),
            pltpu.VMEM((g.Y, (g.HA + 2) * LANES), F32),
            pltpu.VMEM((g.hidden, LANES), F32),
            dma((1,)),
            dma((1,)),
            dma((1,)),
            dma((g.H2,)),
            dma((1,)),
            dma((1,)),
            dma((g.H2,)),
            dma((g.H2,)),
        ],
        compiler_params=pltpu.CompilerParams(
            collective_id=0, has_side_effects=True, vmem_limit_bytes=62 * 1024 * 1024
        ),
    )(feature_a, feature_b, conv_in, bias_in, conv_out, s1, s2)


def solution(mesh):
    in_specs = (P("src", "tgt", None), P("tgt", "src", None), P(), P(), P())
    out_specs = P("tgt", "src", None, None)
    return jax.shard_map(
        per_device, mesh=mesh, in_specs=in_specs, out_specs=out_specs, check_vma=False
    )
```

time: 26.6 us -> 24.6 us (0.925)
  the two profiles are of different devices: /device:TPU:1 before, /device:TPU:0 now
where the time goes in v3:
time: 24.6 us; the launch traced here: 24.4 us
  Pallas kernels  23.1 us (94%)
  local copies, waits for them, and re-layouts  1.38 us (6%)
    pallas_call x1, Pallas kernels, per_device(): pl.pallas_call(functools.partial(kernel, g), out_shape=jax.ShapeDtypeStru...  23.1 us
    unnamed x1, local copies, waits for them, and re-layouts  1.38 us

profile of v3, /device:TPU:0, one launch (start us, length us, event | category | flops | bytes accessed | tf_op | source)
XLA Modules:
  0.0 24.4 jit_solution(16922362735356429005)
XLA Ops:
  0.0 23.1 %shard_map.73 = f32[2,2,16,128]{3,2,1,0:T(8,128)} custom-call(bf16[2,32,1024]{2,1,0:T(8,128)(2,1)} %a_hbm.1, bf16[2,2,1024]{2,1,0:T(2,128)(2,1)} %b_hbm.1, f32[8,81]{1,0:T(8,128)} %cin_hbm.1, f32[8]{0:T(128)} %bias_hbm.1, f32[8,81]{1,0:T(8,128)} %cout_hbm.1, bf16[128,4096]{1,0:T(8,128)(2,1)} %constant.4.clone.s1_hbm, bf16[128,4096]{1,0:T(8,128)(2,1)} %constant.5.clone.s2_hbm), custom_call_target="tpu_custom_call" | custom-call | tf_op jit(solution)/shard_map/pallas_call | solution.py:325
  23.1 1.4 %copy.9 = f32[2,2,16,128]{3,2,1,0:T(8,128)} copy(f32[2,2,16,128]{3,2,1,0:T(8,128)} %shard_map.73) | data formatting | bytes 65536

commit v4 on v3

--- a/solution.py
+++ b/solution.py
@@ -84,8 +84,8 @@
 
 def kernel(
     g, a_hbm, b_hbm, cin_hbm, bias_hbm, cout_hbm, s1_hbm, s2_hbm, out_ref,
-    ach, b_ref, cin_ref, bias_ref, cout_ref, s1_vm, s2_vm, load_sem,
-    bb, bf, vs, vp, r1, r2, u, pat, w1h, w1l, w2h, w2l, y, cpad,
+    ach, cin_ref, bias_ref, cout_ref, s1_vm, s2_vm, load_sem,
+    bb, bf, vs, vp, r1, r2, u, pat, w1, w2, y, cpad,
     s_x, r_x, s_a, r_a, s_b1, s_b2, r_b1, r_b2,
 ):
     S, T = g.S, g.T
@@ -100,7 +100,7 @@
     loads = [
         pltpu.make_async_copy(src, dst, load_sem.at[n])
         for n, (src, dst) in enumerate((
-            (b_hbm, b_ref), (cin_hbm, cin_ref), (bias_hbm, bias_ref), (s1_hbm, s1_vm),
+            (cin_hbm, cin_ref), (bias_hbm, bias_ref), (s1_hbm, s1_vm),
             (cout_hbm, cout_ref), (s2_hbm, s2_vm), (a_hbm, ach.at[core]),
         ))
     ]
@@ -120,7 +120,6 @@
     greet(sibling, t)
     for ph, pt in peers:
         greet(ph * g.G + core, pt)
-    loads[0].wait()
     vp[...] = jnp.zeros(vp.shape, BF16)
     pl.semaphore_wait(barrier, N)
 
@@ -134,12 +133,12 @@
         pltpu.make_async_copy(ref, ref, sem).wait()
 
     for ph, pt in peers:
-        remote(b_ref, bb.at[h, t], s_a.at[0], r_a.at[h], ph * g.G + core, pt).start()
+        remote(b_hbm, bb.at[h, t], s_a.at[0], r_a.at[h], ph * g.G + core, pt).start()
     swap = remote(a_hbm, ach.at[core], s_x.at[0], r_x.at[0], sibling, t)
     swap.start()
-    pltpu.make_async_copy(b_ref, bb.at[h, t], r_a.at[h]).start()
-
-    for load in loads[1:4]:
+    pltpu.make_async_copy(b_hbm, bb.at[h, t], r_a.at[h]).start()
+
+    for load in loads[:3]:
         load.wait()
     cpad[...] = jnp.zeros(cpad.shape, F32)
     cpad[:, : cin_ref.shape[1]] = cin_ref[...]
@@ -171,21 +170,21 @@
             inside = (at_k >= 0) & (at_k < T * g.kb) & (at_l >= 0) & (at_l < S * g.lb)
             block = (block + bias) * jnp.where(inside, 1.0, 0.0).astype(F32)
             at = (k * g.hl + l) * 2 * H
-            w1h[at : at + 2 * H, :] = block[: 2 * H, : g.KP].astype(BF16)
-            w1l[at : at + 2 * H, :] = block[2 * H :, : g.KP].astype(BF16)
-
+            w1[at : at + 2 * H, :] = block[: 2 * H, : g.KP].astype(BF16)
+            w1[g.M + at : g.M + at + 2 * H, :] = block[2 * H :, : g.KP].astype(BF16)
+
+    loads[3].wait()
     loads[4].wait()
-    loads[5].wait()
     cpad[:, : cout_ref.shape[1]] = cout_ref[...]
     taps_h, taps_l = split(cpad[...])
     both = jnp.concatenate([taps_h.astype(F32), taps_l.astype(F32)], axis=0).astype(BF16)
     base = dot(both, s2_vm[...])
     blocks = g.hk * g.hl * 2
-    for first, ref in ((0, w2h), (H, w2l)):
+    for first, at in ((0, 0), (H, g.Y)):
         tall = jnp.concatenate(
             [base[first : first + H, n * LANES : (n + 1) * LANES] for n in range(blocks)], axis=0
         )
-        ref[...] = tall.T[: g.Y].astype(BF16)
+        w2[at : at + g.Y, :] = tall.T[: g.Y].astype(BF16)
 
     tail = g.rows - g.used
     u[:, :, g.used :, :] = jnp.where(
@@ -196,44 +195,53 @@
     y[:, :LANES] = jnp.zeros((g.Y, LANES), F32)
     y[:, (g.HA + 1) * LANES :] = jnp.zeros((g.Y, LANES), F32)
 
-    loads[6].wait()
+    loads[5].wait()
     swap.wait_recv()
-    a = ach[...].astype(F32).reshape(g.pair, g.C)
-    a = jnp.concatenate([a] * (LANES // g.pair), axis=0).astype(BF16)
+    if g.pair == LANES:
+        a = ach[...].reshape(g.pair, g.C)
+    else:
+        a = ach[...].astype(F32).reshape(g.pair, g.C)
+        a = jnp.concatenate([a] * (LANES // g.pair), axis=0).astype(BF16)
+
+    def near(ph, pt):
+        return vp.at[pl.ds(ph + 1, 1), pl.ds(pt, g.bk)]
+
+    def send_near(ph):
+        for m in range(1, T):
+            pt = lax.rem(t + m, T)
+            remote(near(ph, pt), r1.at[h, t], s_b1.at[0], r_b1.at[h], ph * g.G + core, pt).start()
+
+    def send_other(ph):
+        for m in range(T):
+            pt = lax.rem(t + m, T)
+            remote(
+                vp.at[pl.ds(ph + 1 - core, 2), pl.ds(pt, g.bk)], r2.at[h, t], s_b2.at[0],
+                r_b2.at[h], ph * g.G + 1 - core, pt,
+            ).start()
 
     for n in range(H2):
-        ph = lax.rem(h + n, H2)
+        ph = lax.rem(h + H2 - n, H2)
         taken(bb.at[ph], r_a.at[ph])
         for tt in range(T):
             for kk in range(g.kb):
                 at = tt * g.block + kk * g.lb
-                bf[ph, at : at + g.lb, :] = bb[ph, tt, kk].astype(F32)
-
-    total = N * g.block
-    targets = bf[...].reshape(total, g.C).astype(BF16)
-    volume = lax.dot_general(
-        targets, a, (((1,), (1,)), ((), ())), preferred_element_type=F32
-    ) * (g.C ** -0.5)
-    vs[...] = volume.reshape(H2, T * g.block, LANES)
-    for ph in range(H2):
+                bf[n, at : at + g.lb, :] = bb[ph, tt, kk].astype(F32)
+        vs[n] = lax.dot_general(
+            bf[n].astype(BF16), a, (((1,), (1,)), ((), ())), preferred_element_type=F32
+        ) * (g.C ** -0.5)
         for tt in range(T):
-            vp[ph + 1, tt + 1] = vs[ph, tt * g.block : (tt + 1) * g.block, :].astype(BF16)
-
-    def near(ph, pt):
-        return vp.at[pl.ds(ph + 1, 1), pl.ds(pt, g.bk)]
-
-    def other(ph, pt):
-        return vp.at[pl.ds(ph + 1 - core, 2), pl.ds(pt, g.bk)]
-
-    for ph, pt in peers + [(h, t)]:
-        remote(
-            other(ph, pt), r2.at[h, t], s_b2.at[0], r_b2.at[h], ph * g.G + 1 - core, pt
-        ).start()
+            vp[ph + 1, tt + 1] = vs[n, tt * g.block : (tt + 1) * g.block, :].astype(BF16)
+        send_near(ph)
+        if n:
+            remote(
+                near(ph, t), r1.at[h, t], s_b1.at[0], r_b1.at[h], ph * g.G + core, t
+            ).start()
+            send_other(lax.rem(h + H2 - n + core, H2))
+        else:
+            pltpu.make_async_copy(near(h, t), r1.at[h, t], r_b1.at[h]).start()
+    send_other(lax.rem(h + core, H2))
     for ph, pt in peers:
-        remote(near(ph, pt), r1.at[h, t], s_b1.at[0], r_b1.at[h], ph * g.G + core, pt).start()
-    pltpu.make_async_copy(near(h, t), r1.at[h, t], r_b1.at[h]).start()
-    for ph, pt in peers:
-        pltpu.make_async_copy(b_ref, b_ref, s_a.at[0]).wait()
+        pltpu.make_async_copy(b_hbm, b_hbm, s_a.at[0]).wait()
     swap.wait_send()
 
     lane = iota((g.rows, LANES), 1)
@@ -273,11 +281,10 @@
     def filters(n):
         at = LANES + n * wide_n
         patch = pat[:, at : at + wide_n]
-        hid = jnp.maximum(dot(w1h[...], patch) + dot(w1l[...], patch), 0.0)
-        hid_h, hid_l = split(hid)
-        y[:, at : at + wide_n] = (
-            dot(w2h[...], hid_h) + dot(w2l[...], hid_h) + dot(w2h[...], hid_l)
-        )
+        hid = dot(w1[...], patch)
+        hid_h, hid_l = split(jnp.maximum(hid[: g.M] + hid[g.M :], 0.0))
+        res = dot(w2[...], hid_h)
+        y[:, at : at + wide_n] = res[: g.Y] + res[g.Y :] + dot(w2[: g.Y, :], hid_l)
 
     for ph in range(H2):
         taken(r1.at[ph], r_b1.at[ph])
@@ -329,13 +336,12 @@
         out_specs=vm,
         scratch_shapes=[
             pltpu.VMEM((g.G,) + feature_a.shape, BF16),
-            pltpu.VMEM(feature_b.shape, BF16),
             pltpu.VMEM(conv_in.shape, F32),
             pltpu.SMEM(bias_in.shape, F32),
             pltpu.VMEM(conv_out.shape, F32),
             pltpu.VMEM(s1.shape, BF16),
             pltpu.VMEM(s2.shape, BF16),
-            dma((7,)),
+            dma((6,)),
             pltpu.VMEM((g.H2, T, g.kb, g.lb, g.C), BF16),
             pltpu.VMEM((g.H2, T * g.block, g.C), F32),
             pltpu.VMEM((g.H2, T * g.block, LANES), F32),
@@ -344,10 +350,8 @@
             pltpu.VMEM((g.H2, T, 2, g.bk, g.block, LANES), BF16),
             pltpu.VMEM((g.H2, T, g.rows, LANES), F32),
             pltpu.VMEM((g.KP, (g.HA + 2) * LANES), BF16),
-            pltpu.VMEM((g.M, g.KP), BF16),
-            pltpu.VMEM((g.M, g.KP), BF16),
-            pltpu.VMEM((g.Y, g.M), BF16),
-            pltpu.VMEM((g.Y, g.M), BF16),
+            pltpu.VMEM((2 * g.M, g.KP), BF16),
+            pltpu.VMEM((2 * g.Y, g.M), BF16),
             pltpu.VMEM((g.Y, (g.HA + 2) * LANES), F32),
             pltpu.VMEM((g.hidden, LANES), F32),
             dma((1,)),

time: 24.6 us -> 23.8 us (0.967)
  Pallas kernels: 23.1 us -> 22.2 us
    pallas_call x1, Pallas kernels: 23.1 us -> 22.2 us  [per_device(): pl.pallas_call(functools.partial(kernel, g), out_shape=jax.ShapeDtypeStru...]
where the time goes in v4:
time: 23.8 us; the launch traced here: 23.6 us
  Pallas kernels  22.2 us (93%)
  local copies, waits for them, and re-layouts  1.38 us (6%)
    pallas_call x1, Pallas kernels, per_device(): pl.pallas_call(functools.partial(kernel, g), out_shape=jax.ShapeDtypeStru...  22.2 us
    unnamed x1, local copies, waits for them, and re-layouts  1.38 us

profile of v4, /device:TPU:0, one launch (start us, length us, event | category | flops | bytes accessed | tf_op | source)
XLA Modules:
  0.0 23.6 jit_solution(4394977297004885234)
XLA Ops:
  0.0 22.2 %shard_map.73 = f32[2,2,16,128]{3,2,1,0:T(8,128)} custom-call(bf16[2,32,1024]{2,1,0:T(8,128)(2,1)} %a_hbm.1, bf16[2,2,1024]{2,1,0:T(2,128)(2,1)} %b_hbm.1, f32[8,81]{1,0:T(8,128)} %cin_hbm.1, f32[8]{0:T(128)} %bias_hbm.1, f32[8,81]{1,0:T(8,128)} %cout_hbm.1, bf16[128,4096]{1,0:T(8,128)(2,1)} %constant.4.clone.s1_hbm, bf16[128,4096]{1,0:T(8,128)(2,1)} %constant.5.clone.s2_hbm), custom_call_target="tpu_custom_call" | custom-call | tf_op jit(solution)/shard_map/pallas_call | solution.py:332
  22.3 1.4 %copy.9 = f32[2,2,16,128]{3,2,1,0:T(8,128)} copy(f32[2,2,16,128]{3,2,1,0:T(8,128)} %shard_map.73) | data formatting | bytes 65536

commit v5 on v4

--- a/solution.py
+++ b/solution.py
@@ -274,29 +274,42 @@
                     moved = x
                 moved = moved.astype(BF16)
                 for r in range(3):
-                    at = (ph * rows_h + chunk + 2 - r) * LANES
+                    at = pl.multiple_of((ph * rows_h + chunk + 2 - r) * LANES, LANES)
                     first = (r * 3 + sh) * g.KX
-                    pat[first : first + g.KX, at : at + LANES] = moved
-
-    def filters(n):
-        at = LANES + n * wide_n
-        patch = pat[:, at : at + wide_n]
+                    pat[first : first + g.KX, pl.ds(at, LANES)] = moved
+
+    def filters(rows):
+        if not rows:
+            return
+        at = [pl.multiple_of((row + 1) * LANES, LANES) for row in rows]
+        patch = jnp.concatenate([pat[:, pl.ds(place, LANES)] for place in at], axis=1)
         hid = dot(w1[...], patch)
         hid_h, hid_l = split(jnp.maximum(hid[: g.M] + hid[g.M :], 0.0))
         res = dot(w2[...], hid_h)
-        y[:, at : at + wide_n] = res[: g.Y] + res[g.Y :] + dot(w2[: g.Y, :], hid_l)
-
-    for ph in range(H2):
+        res = res[: g.Y] + res[g.Y :] + dot(w2[: g.Y, :], hid_l)
+        for n, place in enumerate(at):
+            y[:, pl.ds(place, LANES)] = res[:, n * LANES : (n + 1) * LANES]
+
+    def inner(ph):
+        filters([ph * rows_h + n for n in range(1, rows_h - 1)])
+
+    def between(ph):
+        row = ph * rows_h + rows_h - 1
+        filters([row, lax.rem(row + 1, g.HA)])
+
+    order = [lax.rem(h + core + n, H2) for n in range(H2)]
+    for n, ph in enumerate(order):
         taken(r1.at[ph], r_b1.at[ph])
         taken(r2.at[ph], r_b2.at[ph])
-    wide_n = 2 * LANES
-    done = 0
-    for ph in range(H2):
+        if n >= 1:
+            inner(order[n - 1])
+        if n >= 2:
+            between(order[n - 2])
         spread(ph)
-        ready = g.HA if ph == H2 - 1 else (ph + 1) * rows_h - 1
-        while (done + 1) * wide_n <= ready * LANES:
-            filters(done)
-            done += 1
+    inner(order[-1])
+    if H2 > 1:
+        between(order[-2])
+    between(order[-1])
 
     last = iota((g.unit, LANES), 1)
     for i in range(g.HA):

time: 23.8 us -> 23 us (0.966)
  the two profiles are of different devices: /device:TPU:0 before, /device:TPU:1 now
where the time goes in v5:
time: 23 us; the launch traced here: 22.8 us
  Pallas kernels  21.5 us (93%)
  local copies, waits for them, and re-layouts  1.38 us (6%)
    pallas_call x1, Pallas kernels, per_device(): pl.pallas_call(functools.partial(kernel, g), out_shape=jax.ShapeDtypeStru...  21.5 us
    unnamed x1, local copies, waits for them, and re-layouts  1.38 us

profile of v5, /device:TPU:1, one launch (start us, length us, event | category | flops | bytes accessed | tf_op | source)
XLA Modules:
  0.0 22.8 jit_solution(5117937272330019813)
XLA Ops:
  0.0 21.5 %shard_map.73 = f32[2,2,16,128]{3,2,1,0:T(8,128)} custom-call(bf16[2,32,1024]{2,1,0:T(8,128)(2,1)} %a_hbm.1, bf16[2,2,1024]{2,1,0:T(2,128)(2,1)} %b_hbm.1, f32[8,81]{1,0:T(8,128)} %cin_hbm.1, f32[8]{0:T(128)} %bias_hbm.1, f32[8,81]{1,0:T(8,128)} %cout_hbm.1, bf16[128,4096]{1,0:T(8,128)(2,1)} %constant.4.clone.s1_hbm, bf16[128,4096]{1,0:T(8,128)(2,1)} %constant.5.clone.s2_hbm), custom_call_target="tpu_custom_call" | custom-call | tf_op jit(solution)/shard_map/pallas_call | solution.py:345
  21.5 1.4 %copy.9 = f32[2,2,16,128]{3,2,1,0:T(8,128)} copy(f32[2,2,16,128]{3,2,1,0:T(8,128)} %shard_map.73) | data formatting | bytes 65536

commit v6 on v5

--- a/solution.py
+++ b/solution.py
@@ -24,7 +24,7 @@
         self.kb, self.lb = b_shape[0], b_shape[1]
         self.hidden = hidden
         self.G = 2
-        assert count_s % self.G == 0
+        assert count_s % self.G == 0 and count_t >= 2
         self.H2 = count_s // self.G
         self.ij = self.rows_i * self.cols_j
         self.HA = self.rows_i * count_s
@@ -97,6 +97,19 @@
     h = s // g.G
     sibling = s + 1 - 2 * core
 
+    barrier = pltpu.get_barrier_semaphore()
+
+    def greet(ps, pt):
+        pl.semaphore_signal(
+            barrier, inc=1, device_id={"src": ps, "tgt": pt}, device_id_type=pl.DeviceIdType.MESH
+        )
+
+    peers = [
+        (lax.rem(h + n, H2), lax.rem(t + m, T)) for n in range(H2) for m in range(T) if n or m
+    ]
+    greet(sibling, t)
+    for ph, pt in peers:
+        greet(ph * g.G + core, pt)
     loads = [
         pltpu.make_async_copy(src, dst, load_sem.at[n])
         for n, (src, dst) in enumerate((
@@ -107,19 +120,6 @@
     for load in loads:
         load.start()
 
-    barrier = pltpu.get_barrier_semaphore()
-
-    def greet(ps, pt):
-        pl.semaphore_signal(
-            barrier, inc=1, device_id={"src": ps, "tgt": pt}, device_id_type=pl.DeviceIdType.MESH
-        )
-
-    peers = [
-        (lax.rem(h + n, H2), lax.rem(t + m, T)) for n in range(H2) for m in range(T) if n or m
-    ]
-    greet(sibling, t)
-    for ph, pt in peers:
-        greet(ph * g.G + core, pt)
     vp[...] = jnp.zeros(vp.shape, BF16)
     pl.semaphore_wait(barrier, N)
 
@@ -203,20 +203,34 @@
         a = ach[...].astype(F32).reshape(g.pair, g.C)
         a = jnp.concatenate([a] * (LANES // g.pair), axis=0).astype(BF16)
 
+    reach = [slice(1 if pt == 0 else 0, g.bk - 1 if pt == T - 1 else g.bk) for pt in range(T)]
+    rows_t = sorted(range(T), key=lambda pt: min(pt, T - 1 - pt))
+    at_edge = (t == 0) | (t == T - 1)
+
+    @pl.when(t == 0)
+    def _():
+        r1[:, :, :, 0] = jnp.zeros((H2, T, 1, g.block, LANES), BF16)
+        r2[:, :, :, 0] = jnp.zeros((H2, T, 2, g.block, LANES), BF16)
+
+    @pl.when(t == T - 1)
+    def _():
+        r1[:, :, :, g.bk - 1] = jnp.zeros((H2, T, 1, g.block, LANES), BF16)
+        r2[:, :, :, g.bk - 1] = jnp.zeros((H2, T, 2, g.block, LANES), BF16)
+
+    def source(first, count, pt):
+        return vp.at[pl.ds(first, count), pt + reach[pt].start : pt + reach[pt].stop]
+
     def near(ph, pt):
-        return vp.at[pl.ds(ph + 1, 1), pl.ds(pt, g.bk)]
-
-    def send_near(ph):
-        for m in range(1, T):
-            pt = lax.rem(t + m, T)
-            remote(near(ph, pt), r1.at[h, t], s_b1.at[0], r_b1.at[h], ph * g.G + core, pt).start()
+        return remote(
+            source(ph + 1, 1, pt), r1.at[h, t, :, reach[pt]], s_b1.at[0], r_b1.at[h],
+            ph * g.G + core, pt,
+        )
 
     def send_other(ph):
-        for m in range(T):
-            pt = lax.rem(t + m, T)
+        for pt in rows_t:
             remote(
-                vp.at[pl.ds(ph + 1 - core, 2), pl.ds(pt, g.bk)], r2.at[h, t], s_b2.at[0],
-                r_b2.at[h], ph * g.G + 1 - core, pt,
+                source(ph + 1 - core, 2, pt), r2.at[h, t, :, reach[pt]], s_b2.at[0], r_b2.at[h],
+                ph * g.G + 1 - core, pt,
             ).start()
 
     for n in range(H2):
@@ -231,14 +245,23 @@
         ) * (g.C ** -0.5)
         for tt in range(T):
             vp[ph + 1, tt + 1] = vs[n, tt * g.block : (tt + 1) * g.block, :].astype(BF16)
-        send_near(ph)
+        for pt in rows_t:
+            if n:
+                near(ph, pt).start()
+                continue
+
+            @pl.when(t != pt)
+            def _():
+                near(ph, pt).start()
+
+            @pl.when(t == pt)
+            def _():
+                pltpu.make_async_copy(
+                    source(h + 1, 1, pt), r1.at[h, t, :, reach[pt]], r_b1.at[h]
+                ).start()
+
         if n:
-            remote(
-                near(ph, t), r1.at[h, t], s_b1.at[0], r_b1.at[h], ph * g.G + core, t
-            ).start()
             send_other(lax.rem(h + H2 - n + core, H2))
-        else:
-            pltpu.make_async_copy(near(h, t), r1.at[h, t], r_b1.at[h]).start()
     send_other(lax.rem(h + core, H2))
     for ph, pt in peers:
         pltpu.make_async_copy(b_hbm, b_hbm, s_a.at[0]).wait()
@@ -297,41 +320,69 @@
         row = ph * rows_h + rows_h - 1
         filters([row, lax.rem(row + 1, g.HA)])
 
+    last = iota((g.unit, LANES), 1)
+
+    def finish(ph):
+        for n in range(rows_h):
+            i = ph * rows_h + n
+            sums = []
+            for sh in range(3):
+                part = None
+                for r in range(3):
+                    first = (r * 3 + sh) * g.unit
+                    at = pl.multiple_of((i + r) * LANES, LANES)
+                    term = y[first : first + g.unit, pl.ds(at, LANES)]
+                    part = term if part is None else part + term
+                sums.append(part)
+            res = sums[1]
+            res = res + jnp.where(last == 0, 0.0, pltpu.roll(sums[0], 1, 1))
+            res = res + jnp.where(last == LANES - 1, 0.0, pltpu.roll(sums[2], LANES - 1, 1))
+            for k in range(g.kb):
+                for l in range(g.lb):
+                    m = k * g.lb + l
+                    out_ref[k, l, pl.ds(i, 1), :] = res[m : m + 1, :]
+
     order = [lax.rem(h + core + n, H2) for n in range(H2)]
+    edge = slice(0, g.bk - 1)
     for n, ph in enumerate(order):
-        taken(r1.at[ph], r_b1.at[ph])
-        taken(r2.at[ph], r_b2.at[ph])
+
+        @pl.when(at_edge)
+        def _():
+            taken(r1.at[ph, :, :, edge], r_b1.at[ph])
+            taken(r2.at[ph, :, :, edge], r_b2.at[ph])
+
+        @pl.when(jnp.logical_not(at_edge))
+        def _():
+            taken(r1.at[ph], r_b1.at[ph])
+            taken(r2.at[ph], r_b2.at[ph])
+
         if n >= 1:
             inner(order[n - 1])
         if n >= 2:
             between(order[n - 2])
+        if n >= 3:
+            finish(order[n - 2])
         spread(ph)
     inner(order[-1])
     if H2 > 1:
         between(order[-2])
     between(order[-1])
-
-    last = iota((g.unit, LANES), 1)
-    for i in range(g.HA):
-        sums = []
-        for sh in range(3):
-            part = None
-            for r in range(3):
-                first = (r * 3 + sh) * g.unit
-                term = y[first : first + g.unit, (i + r) * LANES : (i + r + 1) * LANES]
-                part = term if part is None else part + term
-            sums.append(part)
-        res = sums[1]
-        res = res + jnp.where(last == 0, 0.0, pltpu.roll(sums[0], 1, 1))
-        res = res + jnp.where(last == LANES - 1, 0.0, pltpu.roll(sums[2], LANES - 1, 1))
-        for k in range(g.kb):
-            for l in range(g.lb):
-                n = k * g.lb + l
-                out_ref[k, l, i : i + 1, :] = res[n : n + 1, :]
-
-    taken(r2, s_b2.at[0])
-    for ph, pt in peers:
-        pltpu.make_async_copy(r1.at[0, 0], r1.at[0, 0], s_b1.at[0]).wait()
+    for n in range(H2):
+        if n == 0 or n >= max(H2 - 2, 1):
+            finish(order[n])
+
+    taken(r2.at[:, 1 : T - 1], s_b2.at[0])
+    taken(r2.at[:, :2, :, edge], s_b2.at[0])
+    for n in range(H2):
+        for pt in range(T):
+            part = r1.at[0, 0, :, reach[pt]]
+            if n:
+                taken(part, s_b1.at[0])
+                continue
+
+            @pl.when(t != pt)
+            def _():
+                taken(part, s_b1.at[0])
 
 
 def per_device(feature_a, feature_b, conv_in, bias_in, conv_out):

time: 23 us -> 23 us (level)
  no operation moved by 1% of the time
where the time goes in v6:
time: 23 us; the launch traced here: 22.8 us
  Pallas kernels  21.4 us (93%)
  local copies, waits for them, and re-layouts  1.38 us (6%)
    pallas_call x1, Pallas kernels, per_device(): pl.pallas_call(functools.partial(kernel, g), out_shape=jax.ShapeDtypeStru...  21.4 us
    unnamed x1, local copies, waits for them, and re-layouts  1.38 us

profile of v6, /device:TPU:1, one launch (start us, length us, event | category | flops | bytes accessed | tf_op | source)
XLA Modules:
  0.0 22.8 jit_solution(11019948464092736477)
XLA Ops:
  0.0 21.4 %shard_map.73 = f32[2,2,16,128]{3,2,1,0:T(8,128)} custom-call(bf16[2,32,1024]{2,1,0:T(8,128)(2,1)} %a_hbm.1, bf16[2,2,1024]{2,1,0:T(2,128)(2,1)} %b_hbm.1, f32[8,81]{1,0:T(8,128)} %cin_hbm.1, f32[8]{0:T(128)} %bias_hbm.1, f32[8,81]{1,0:T(8,128)} %cout_hbm.1, bf16[128,4096]{1,0:T(8,128)(2,1)} %constant.4.clone.s1_hbm, bf16[128,4096]{1,0:T(8,128)(2,1)} %constant.5.clone.s2_hbm), custom_call_target="tpu_custom_call" | custom-call | tf_op jit(solution)/shard_map/pallas_call | solution.py:396
  21.4 1.4 %copy.9 = f32[2,2,16,128]{3,2,1,0:T(8,128)} copy(f32[2,2,16,128]{3,2,1,0:T(8,128)} %shard_map.73) | data formatting | bytes 65536

commit v7 on v6

--- a/solution.py
+++ b/solution.py
@@ -170,8 +170,102 @@
             inside = (at_k >= 0) & (at_k < T * g.kb) & (at_l >= 0) & (at_l < S * g.lb)
             block = (block + bias) * jnp.where(inside, 1.0, 0.0).astype(F32)
             at = (k * g.hl + l) * 2 * H
-            w1[at : at + 2 * H, :] = block[: 2 * H, : g.KP].astype(BF16)
-            w1[g.M + at : g.M + at + 2 * H, :] = block[2 * H :, : g.KP].astype(BF16)
+            w1[at : at + 2 * H, :] = block[: 2 * H].astype(BF16)
+            w1[g.M + at : g.M + at + 2 * H, :] = block[2 * H :].astype(BF16)
+
+    tail = g.rows - g.used
+    u[:, :, g.used :, :] = jnp.where(
+        iota((H2, T, tail, LANES), 2) == tail - 1, jnp.ones((H2, T, tail, LANES), F32), 0.0
+    )
+    pat[: 3 * g.KX, LANES : 2 * LANES] = jnp.zeros((3 * g.KX, LANES), BF16)
+    if g.KW > g.KP:
+        pat[g.KP :, :] = jnp.zeros((g.KW - g.KP, (g.HA + 2) * LANES), BF16)
+    pat[6 * g.KX : g.KP, g.HA * LANES : (g.HA + 1) * LANES] = jnp.zeros((3 * g.KX, LANES), BF16)
+    y[:, :LANES] = jnp.zeros((g.Y, LANES), F32)
+    y[:, (g.HA + 1) * LANES :] = jnp.zeros((g.Y, LANES), F32)
+
+    loads[5].wait()
+    swap.wait_recv()
+    if g.pair == LANES:
+        a = ach[...].reshape(g.pair, g.C)
+    else:
+        a = ach[...].astype(F32).reshape(g.pair, g.C)
+        a = jnp.concatenate([a] * (LANES // g.pair), axis=0).astype(BF16)
+
+    reach = [slice(1 if pt == 0 else 0, g.bk - 1 if pt == T - 1 else g.bk) for pt in range(T)]
+    rows_t = sorted(range(T), key=lambda pt: min(pt, T - 1 - pt))
+    at_edge = (t == 0) | (t == T - 1)
+
+    @pl.when(t == 0)
+    def _():
+        r1[:, :, :, 0] = jnp.zeros((H2, T, 1, g.block, LANES), BF16)
+        r2[:, :, :, 0] = jnp.zeros((H2, T, 2, g.block, LANES), BF16)
+
+    @pl.when(t == T - 1)
+    def _():
+        r1[:, :, :, g.bk - 1] = jnp.zeros((H2, T, 1, g.block, LANES), BF16)
+        r2[:, :, :, g.bk - 1] = jnp.zeros((H2, T, 2, g.block, LANES), BF16)
+
+    def source(first, count, pt):
+        return vp.at[pl.ds(first, count), pt + reach[pt].start : pt + reach[pt].stop]
+
+    def near(ph, pt):
+        return remote(
+            source(ph + 1, 1, pt), r1.at[h, t, :, reach[pt]], s_b1.at[0], r_b1.at[h],
+            ph * g.G + core, pt,
+        )
+
+    def send_other(ph):
+        for pt in rows_t:
+            remote(
+                source(ph + 1 - core, 2, pt), r2.at[h, t, :, reach[pt]], s_b2.at[0], r_b2.at[h],
+                ph * g.G + 1 - core, pt,
+            ).start()
+
+    def columns(steps):
+        rows = T * g.block
+        for n in steps:
+            ph = lax.rem(h + H2 - n, H2)
+            taken(bb.at[ph], r_a.at[ph])
+            for tt in range(T):
+                for kk in range(g.kb):
+                    at = tt * g.block + kk * g.lb
+                    bf[n, at : at + g.lb, :] = bb[ph, tt, kk].astype(F32)
+        first, count = steps[0], len(steps)
+        targets = bf[first : first + count].reshape(count * rows, g.C).astype(BF16)
+        scores = lax.dot_general(
+            targets, a, (((1,), (1,)), ((), ())), preferred_element_type=F32
+        ) * (g.C ** -0.5)
+        vs[first : first + count] = scores.reshape(count, rows, LANES)
+        for n in steps:
+            ph = lax.rem(h + H2 - n, H2)
+            for tt in range(T):
+                vp[ph + 1, tt + 1] = vs[n, tt * g.block : (tt + 1) * g.block, :].astype(BF16)
+        for n in steps:
+            ph = lax.rem(h + H2 - n, H2)
+            for pt in rows_t:
+                if n:
+                    near(ph, pt).start()
+                    continue
+
+                @pl.when(t != pt)
+                def _():
+                    near(ph, pt).start()
+
+                @pl.when(t == pt)
+                def _():
+                    pltpu.make_async_copy(
+                        source(h + 1, 1, pt), r1.at[h, t, :, reach[pt]], r_b1.at[h]
+                    ).start()
+
+            if n:
+                send_other(lax.rem(h + H2 - n + core, H2))
+
+    half = -(-H2 // 2)
+    columns(range(half))
+    if half < H2:
+        columns(range(half, H2))
+    send_other(lax.rem(h + core, H2))
 
     loads[3].wait()
     loads[4].wait()
@@ -186,83 +280,6 @@
         )
         w2[at : at + g.Y, :] = tall.T[: g.Y].astype(BF16)
 
-    tail = g.rows - g.used
-    u[:, :, g.used :, :] = jnp.where(
-        iota((H2, T, tail, LANES), 2) == tail - 1, jnp.ones((H2, T, tail, LANES), F32), 0.0
-    )
-    pat[: 3 * g.KX, LANES : 2 * LANES] = jnp.zeros((3 * g.KX, LANES), BF16)
-    pat[6 * g.KX :, g.HA * LANES : (g.HA + 1) * LANES] = jnp.zeros((3 * g.KX, LANES), BF16)
-    y[:, :LANES] = jnp.zeros((g.Y, LANES), F32)
-    y[:, (g.HA + 1) * LANES :] = jnp.zeros((g.Y, LANES), F32)
-
-    loads[5].wait()
-    swap.wait_recv()
-    if g.pair == LANES:
-        a = ach[...].reshape(g.pair, g.C)
-    else:
-        a = ach[...].astype(F32).reshape(g.pair, g.C)
-        a = jnp.concatenate([a] * (LANES // g.pair), axis=0).astype(BF16)
-
-    reach = [slice(1 if pt == 0 else 0, g.bk - 1 if pt == T - 1 else g.bk) for pt in range(T)]
-    rows_t = sorted(range(T), key=lambda pt: min(pt, T - 1 - pt))
-    at_edge = (t == 0) | (t == T - 1)
-
-    @pl.when(t == 0)
-    def _():
-        r1[:, :, :, 0] = jnp.zeros((H2, T, 1, g.block, LANES), BF16)
-        r2[:, :, :, 0] = jnp.zeros((H2, T, 2, g.block, LANES), BF16)
-
-    @pl.when(t == T - 1)
-    def _():
-        r1[:, :, :, g.bk - 1] = jnp.zeros((H2, T, 1, g.block, LANES), BF16)
-        r2[:, :, :, g.bk - 1] = jnp.zeros((H2, T, 2, g.block, LANES), BF16)
-
-    def source(first, count, pt):
-        return vp.at[pl.ds(first, count), pt + reach[pt].start : pt + reach[pt].stop]
-
-    def near(ph, pt):
-        return remote(
-            source(ph + 1, 1, pt), r1.at[h, t, :, reach[pt]], s_b1.at[0], r_b1.at[h],
-            ph * g.G + core, pt,
-        )
-
-    def send_other(ph):
-        for pt in rows_t:
-            remote(
-                source(ph + 1 - core, 2, pt), r2.at[h, t, :, reach[pt]], s_b2.at[0], r_b2.at[h],
-                ph * g.G + 1 - core, pt,
-            ).start()
-
-    for n in range(H2):
-        ph = lax.rem(h + H2 - n, H2)
-        taken(bb.at[ph], r_a.at[ph])
-        for tt in range(T):
-            for kk in range(g.kb):
-                at = tt * g.block + kk * g.lb
-                bf[n, at : at + g.lb, :] = bb[ph, tt, kk].astype(F32)
-        vs[n] = lax.dot_general(
-            bf[n].astype(BF16), a, (((1,), (1,)), ((), ())), preferred_element_type=F32
-        ) * (g.C ** -0.5)
-        for tt in range(T):
-            vp[ph + 1, tt + 1] = vs[n, tt * g.block : (tt + 1) * g.block, :].astype(BF16)
-        for pt in rows_t:
-            if n:
-                near(ph, pt).start()
-                continue
-
-            @pl.when(t != pt)
-            def _():
-                near(ph, pt).start()
-
-            @pl.when(t == pt)
-            def _():
-                pltpu.make_async_copy(
-                    source(h + 1, 1, pt), r1.at[h, t, :, reach[pt]], r_b1.at[h]
-                ).start()
-
-        if n:
-            send_other(lax.rem(h + H2 - n + core, H2))
-    send_other(lax.rem(h + core, H2))
     for ph, pt in peers:
         pltpu.make_async_copy(b_hbm, b_hbm, s_a.at[0]).wait()
     swap.wait_send()
@@ -413,8 +430,8 @@
             pltpu.VMEM((g.H2, T, 1, g.bk, g.block, LANES), BF16),
             pltpu.VMEM((g.H2, T, 2, g.bk, g.block, LANES), BF16),
             pltpu.VMEM((g.H2, T, g.rows, LANES), F32),
-            pltpu.VMEM((g.KP, (g.HA + 2) * LANES), BF16),
-            pltpu.VMEM((2 * g.M, g.KP), BF16),
+            pltpu.VMEM((g.KW, (g.HA + 2) * LANES), BF16),
+            pltpu.VMEM((2 * g.M, g.KW), BF16),
             pltpu.VMEM((2 * g.Y, g.M), BF16),
             pltpu.VMEM((g.Y, (g.HA + 2) * LANES), F32),
             pltpu.VMEM((g.hidden, LANES), F32),

time: 23 us -> 23.2 us (level)
  no operation moved by 1% of the time
where the time goes in v7:
time: 23.2 us; the launch traced here: 23 us
  Pallas kernels  21.6 us (93%)
  local copies, waits for them, and re-layouts  1.38 us (6%)
    pallas_call x1, Pallas kernels, per_device(): pl.pallas_call(functools.partial(kernel, g), out_shape=jax.ShapeDtypeStru...  21.6 us
    unnamed x1, local copies, waits for them, and re-layouts  1.38 us

profile of v7, /device:TPU:1, one launch (start us, length us, event | category | flops | bytes accessed | tf_op | source)
XLA Modules:
  0.0 23.0 jit_solution(16748773759117837004)
XLA Ops:
  0.0 21.6 %shard_map.73 = f32[2,2,16,128]{3,2,1,0:T(8,128)} custom-call(bf16[2,32,1024]{2,1,0:T(8,128)(2,1)} %a_hbm.1, bf16[2,2,1024]{2,1,0:T(2,128)(2,1)} %b_hbm.1, f32[8,81]{1,0:T(8,128)} %cin_hbm.1, f32[8]{0:T(128)} %bias_hbm.1, f32[8,81]{1,0:T(8,128)} %cout_hbm.1, bf16[128,4096]{1,0:T(8,128)(2,1)} %constant.4.clone.s1_hbm, bf16[128,4096]{1,0:T(8,128)(2,1)} %constant.5.clone.s2_hbm), custom_call_target="tpu_custom_call" | custom-call | tf_op jit(solution)/shard_map/pallas_call | solution.py:413
  21.6 1.4 %copy.9 = f32[2,2,16,128]{3,2,1,0:T(8,128)} copy(f32[2,2,16,128]{3,2,1,0:T(8,128)} %shard_map.73) | data formatting | bytes 65536

commit v8 on v6

--- a/solution.py
+++ b/solution.py
@@ -342,7 +342,7 @@
                     m = k * g.lb + l
                     out_ref[k, l, pl.ds(i, 1), :] = res[m : m + 1, :]
 
-    order = [lax.rem(h + core + n, H2) for n in range(H2)]
+    order = [lax.rem(h + n, H2) for n in range(H2)]
     edge = slice(0, g.bk - 1)
     for n, ph in enumerate(order):
 

time: 23 us -> 22.4 us (0.974)
  Pallas kernels: 21.4 us -> 20.7 us
    pallas_call x1, Pallas kernels: 21.4 us -> 20.7 us  [per_device(): pl.pallas_call(functools.partial(kernel, g), out_shape=jax.ShapeDtypeStru...]
where the time goes in v8:
time: 22.4 us; the launch traced here: 22.1 us
  Pallas kernels  20.7 us (92%)
  local copies, waits for them, and re-layouts  1.38 us (6%)
    pallas_call x1, Pallas kernels, per_device(): pl.pallas_call(functools.partial(kernel, g), out_shape=jax.ShapeDtypeStru...  20.7 us
    unnamed x1, local copies, waits for them, and re-layouts  1.38 us

profile of v8, /device:TPU:1, one launch (start us, length us, event | category | flops | bytes accessed | tf_op | source)
XLA Modules:
  0.0 22.1 jit_solution(6631741188186916296)
XLA Ops:
  0.0 20.7 %shard_map.73 = f32[2,2,16,128]{3,2,1,0:T(8,128)} custom-call(bf16[2,32,1024]{2,1,0:T(8,128)(2,1)} %a_hbm.1, bf16[2,2,1024]{2,1,0:T(2,128)(2,1)} %b_hbm.1, f32[8,81]{1,0:T(8,128)} %cin_hbm.1, f32[8]{0:T(128)} %bias_hbm.1, f32[8,81]{1,0:T(8,128)} %cout_hbm.1, bf16[128,4096]{1,0:T(8,128)(2,1)} %constant.4.clone.s1_hbm, bf16[128,4096]{1,0:T(8,128)(2,1)} %constant.5.clone.s2_hbm), custom_call_target="tpu_custom_call" | custom-call | tf_op jit(solution)/shard_map/pallas_call | solution.py:396
  20.7 1.4 %copy.9 = f32[2,2,16,128]{3,2,1,0:T(8,128)} copy(f32[2,2,16,128]{3,2,1,0:T(8,128)} %shard_map.73) | data formatting | bytes 65536

commit v9 on v8

--- a/solution.py
+++ b/solution.py
@@ -345,23 +345,23 @@
     order = [lax.rem(h + n, H2) for n in range(H2)]
     edge = slice(0, g.bk - 1)
     for n, ph in enumerate(order):
-
-        @pl.when(at_edge)
-        def _():
-            taken(r1.at[ph, :, :, edge], r_b1.at[ph])
-            taken(r2.at[ph, :, :, edge], r_b2.at[ph])
-
-        @pl.when(jnp.logical_not(at_edge))
-        def _():
-            taken(r1.at[ph], r_b1.at[ph])
-            taken(r2.at[ph], r_b2.at[ph])
-
         if n >= 1:
             inner(order[n - 1])
         if n >= 2:
             between(order[n - 2])
         if n >= 3:
             finish(order[n - 2])
+
+        @pl.when(at_edge)
+        def _():
+            taken(r1.at[ph, :, :, edge], r_b1.at[ph])
+            taken(r2.at[ph, :, :, edge], r_b2.at[ph])
+
+        @pl.when(jnp.logical_not(at_edge))
+        def _():
+            taken(r1.at[ph], r_b1.at[ph])
+            taken(r2.at[ph], r_b2.at[ph])
+
         spread(ph)
     inner(order[-1])
     if H2 > 1:

time: 22.4 us -> 23.2 us (1.036)
  Pallas kernels: 20.7 us -> 21.6 us
    pallas_call x1, Pallas kernels: 20.7 us -> 21.6 us  [per_device(): pl.pallas_call(functools.partial(kernel, g), out_shape=jax.ShapeDtypeStru...]
where the time goes in v9:
time: 23.2 us; the launch traced here: 23 us
  Pallas kernels  21.6 us (93%)
  local copies, waits for them, and re-layouts  1.38 us (6%)
    pallas_call x1, Pallas kernels, per_device(): pl.pallas_call(functools.partial(kernel, g), out_shape=jax.ShapeDtypeStru...  21.6 us
    unnamed x1, local copies, waits for them, and re-layouts  1.38 us

profile of v9, /device:TPU:1, one launch (start us, length us, event | category | flops | bytes accessed | tf_op | source)
XLA Modules:
  0.0 23.0 jit_solution(13585867322668445294)
XLA Ops:
  0.0 21.6 %shard_map.73 = f32[2,2,16,128]{3,2,1,0:T(8,128)} custom-call(bf16[2,32,1024]{2,1,0:T(8,128)(2,1)} %a_hbm.1, bf16[2,2,1024]{2,1,0:T(2,128)(2,1)} %b_hbm.1, f32[8,81]{1,0:T(8,128)} %cin_hbm.1, f32[8]{0:T(128)} %bias_hbm.1, f32[8,81]{1,0:T(8,128)} %cout_hbm.1, bf16[128,4096]{1,0:T(8,128)(2,1)} %constant.4.clone.s1_hbm, bf16[128,4096]{1,0:T(8,128)(2,1)} %constant.5.clone.s2_hbm), custom_call_target="tpu_custom_call" | custom-call | tf_op jit(solution)/shard_map/pallas_call | solution.py:396
  21.6 1.4 %copy.9 = f32[2,2,16,128]{3,2,1,0:T(8,128)} copy(f32[2,2,16,128]{3,2,1,0:T(8,128)} %shard_map.73) | data formatting | bytes 65536
